TPU v7x, 32 devices: a whole 2x2x4 slice. The times are simulated.
32 devices in a mesh: sky: 8 (over z, x), vel: 4 (over y, core).
Axes of the slice: x: 2, y: 2, z: 4, core: 2. Of those that a mesh axis runs over, the one named last changes fastest.
Arguments:
- psi: float32 [4, 1024, 2048], P(None, 'sky', 'vel'), may hold values from -6 to 6
- phi: float32 [4, 1024, 2048], P(None, 'sky', 'vel'), may hold values from 0.25 to 4
- mask: int32 [4, 1024, 2048], P(None, 'sky', 'vel'), may hold values 0 or 1
- velocities: int32 [32, 2], replicated, may hold values from -12 to 12, as said below
- time_offsets: int32 [4], replicated, may hold values from 0 to 8, as said below
Outputs:
- likelihood: float32 [32, 1024, 2048], P('vel', 'sky')
Inputs may be any that keep to these rules, and one draw needn't show every extreme that they name: `velocities`: every component lies in -12 .. 12. `time_offsets`: the first exposure's offset is 0.
All inputs are finite; a program needn't handle non-finite values. No bound on the sum of `mask` on one device may be relied on, other than what follows from the above.
Results may differ from a plain program's by a relative error of at most 0.0003.
Values sent between devices are 32-bit elements; how exact they have to be, the bound alone decides.
A program may use at most 128 MiB of HBM per device.

v0:
```python
import jax
import jax.numpy as jnp
from jax import lax
from jax.sharding import PartitionSpec as P

HALO = 25


def padded_2(block, sides, width):
    for axis, dim in sides:
        count = lax.axis_size(axis)
        forward = [(i, i + 1) for i in range(count - 1)]
        backward = [(target, source) for source, target in forward]
        low = lax.ppermute(
            lax.slice_in_dim(block, block.shape[dim] - width, None, axis=dim), axis, forward
        )
        high = lax.ppermute(lax.slice_in_dim(block, 0, width, axis=dim), axis, backward)
        block = jnp.concatenate([low, block, high], axis=dim)
    return block


def stack_maps(padded, velocity, time_offsets, rows, cols):
    total = jnp.zeros((2, rows, cols), jnp.float32)
    for exposure in range(padded.shape[0]):
        shift_row = velocity[0] * time_offsets[exposure]
        shift_col = velocity[1] * time_offsets[exposure]
        whole_row = jnp.floor_divide(shift_row, 4)
        whole_col = jnp.floor_divide(shift_col, 4)
        frac_row = (shift_row - 4 * whole_row).astype(jnp.float32) * 0.25
        frac_col = (shift_col - 4 * whole_col).astype(jnp.float32) * 0.25
        layer = padded[exposure]
        row_start = HALO + whole_row
        col_start = HALO + whole_col
        zero_index = jnp.int32(0)
        top_left = lax.dynamic_slice(layer, (zero_index, row_start, col_start), (2, rows, cols))
        top_right = lax.dynamic_slice(
            layer, (zero_index, row_start, col_start + 1), (2, rows, cols)
        )
        low_left = lax.dynamic_slice(layer, (zero_index, row_start + 1, col_start), (2, rows, cols))
        low_right = lax.dynamic_slice(
            layer, (zero_index, row_start + 1, col_start + 1), (2, rows, cols)
        )
        upper = (1.0 - frac_col) * top_left + frac_col * top_right
        lower = (1.0 - frac_col) * low_left + frac_col * low_right
        total = total + ((1.0 - frac_row) * upper + frac_row * lower)
    return total[0] / jnp.sqrt(jnp.maximum(total[1], 1.0))


def pad_right(block, cols):
    needed = cols + 2 * HALO
    target = (needed + 127) // 128 * 128
    have = block.shape[3] + HALO
    return jnp.pad(block, ((0, 0), (0, 0), (0, 0), (HALO, target - have)))


def body(psi, phi, mask, velocities, time_offsets):
    keep = mask == 0
    stacked = jnp.stack([jnp.where(keep, psi, 0.0), jnp.where(keep, phi, 0.0)], axis=1)
    rows = psi.shape[1]
    per_device = velocities.shape[0] // lax.axis_size("vel")
    with_rim = padded_2(stacked, (("sky", 2),), HALO)
    whole_rows = lax.all_gather(with_rim, "vel", axis=3, tiled=True)
    full_cols = whole_rows.shape[3]
    padded = pad_right(whole_rows, full_cols)
    own_velocities = lax.dynamic_slice_in_dim(
        velocities, lax.axis_index("vel") * per_device, per_device, 0
    )

    def own_velocity(velocity):
        return stack_maps(padded, velocity, time_offsets, rows, full_cols)

    return lax.map(own_velocity, own_velocities)


def solution(mesh):
    return jax.shard_map(
        body,
        mesh=mesh,
        in_specs=(P(None, "sky", "vel"), P(None, "sky", "vel"), P(None, "sky", "vel"), P(), P()),
        out_specs=P("vel", "sky", None),
        check_vma=False,
    )
```

profile of v0, /device:TPU:0, one launch (start us, length us, event | category | flops | bytes accessed | tf_op | source)
XLA Modules:
  0.0 456.9 jit_solution(2926945281676351086)
XLA Ops:
  6.5 1.9 select_bitcast_fusion.1
  8.9 4.9 %collective-permute-start = (f32[4,2,25,512]{3,2,1,0:T(8,128)S(1)}, f32[4,2,25,512]{3,2,1,0:T(8,128)S(1)}, u32[]{:S(2)}, u32[]{:S(2)}) collective-permute-start(f32[4,2,25,512]{3,2,1,0:T(8,128)S(1)} %get-tuple-element.197), channel_id=1, source_target_pairs={{0,4},{4,8},{8,12},{12,16},{16,20},{20,24},{24,28},{1,5},{5,9},{9,... | collective-permute-start | bytes 1228808 | tf_op jit(solution)/shard_map/ppermute | solution.py:14
  13.7 1.3 collective-permute-start.1
  15.0 21.1 %collective-permute-done = f32[4,2,25,512]{3,2,1,0:T(8,128)S(1)} collective-permute-done((f32[4,2,25,512]{3,2,1,0:T(8,128)S(1)}, f32[4,2,25,512]{3,2,1,0:T(8,128)S(1)}, u32[]{:S(2)}, u32[]{:S(2)}) %collective-permute-start) | collective-permute-done | bytes 409632 | tf_op jit(solution)/shard_map/ppermute | solution.py:14
  36.1 2.2 pad_maximum_fusion
  38.4 81.4 %all-gather.2.cloned.1.call-done = f32[4,2,178,2048]{3,2,1,0:T(8,128)} async-done(((f32[4,2,178,512]{3,2,1,0:T(8,128)}), f32[4,2,178,2048]{3,2,1,0:T(8,128)}) %all-gather.2.cloned.1.call-update) | async-done | bytes 11665424 | tf_op jit(solution)/shard_map/all_gather | solution.py:62
  119.8 12.4 %pad.4 = f32[4,2,178,2176]{3,2,1,0:T(8,128)} pad(f32[4,2,178,2048]{3,2,1,0:T(8,128)} %all-gather.2.cloned.1.call-done, f32[]{:T(128)} %constant.265.clone.1), padding=0_0x0_0x0_0x25_103 | pad | bytes 24059908 | tf_op jit(solution)/shard_map/jit(_pad)/pad | solution.py:53
  132.2 317.9 %while.15 = (s32[]{:T(128)}, f32[8,128,2048]{2,1,0:T(8,128)}, s32[8,2]{0,1:T(2,128)S(1)}, s32[4]{0:T(128)S(1)}, f32[4,2,178,2176]{3,2,1,0:T(8,128)}, /*index=5*/...) while((s32[]{:T(128)}, f32[8,128,2048]{2,1,0:T(8,128)}, ...), condition=%wide.region_1.2_spmd, body=%wide.region_0.1_spmd.sunk | while | flops 20971752 | bytes 63589584 | solution.py:72
  132.3 0.6 fusion.12
  132.9 0.6 fusion.13
  143.4 8.6 %fusion.11 = (f32[1,2,178,2176]{3,2,1,0:T(8,128)S(1)}, f32[1,2,178,2176]{3,2,1,0:T(8,128)}, f32[1,2,178,2176]{3,2,1,0:T(8,128)}, f32[1,2,178,2176]{3,2,1,0:T(8,128)}) fusion(f32[4,2,178,2176]{3,2,1,0:T(8,128)} %get-tuple-element.292), kind=kLoop, calls=%fused_computation.14.clone.1 | loop fusion | bytes 24788992 | tf_op jit(solution)/shard_map/while/body/eval_jaxpr/slice | solution.py:31
  152.0 18.9 %add_add_fusion.2 = f32[1,2,128,2048]{3,2,1,0:T(8,128)S(1)} fusion(f32[1,2,178,2176]{3,2,1,0:T(8,128)} %get-tuple-element.240, s32[]{:T(128)S(6)} %select_n.298, s32[]{:T(128)S(6)} %select_n.300, s32[]{:T(128)S(6)} %select_n.301, s32[]{:T(128)S(6)} %select_n.302, f32[1,2,178,2176]{3,2,1,0:T(8,128)} %get-tuple-element.244, s32[]{:T(128)S(6)} %select_n.304, ...), kind=kLoop, calls=%fused_computation.clone.1 | loop fusion | flops 20447232 | bytes 35651712 | tf_op jit(solution)/shard_map/while/body/eval_jaxpr/add | solution.py:45
  170.9 1.2 fusion.14
  172.2 0.6 fusion.12
  172.7 0.6 fusion.13
  183.3 8.6 %fusion.11 = (f32[1,2,178,2176]{3,2,1,0:T(8,128)S(1)}, f32[1,2,178,2176]{3,2,1,0:T(8,128)}, f32[1,2,178,2176]{3,2,1,0:T(8,128)}, f32[1,2,178,2176]{3,2,1,0:T(8,128)}) fusion(f32[4,2,178,2176]{3,2,1,0:T(8,128)} %get-tuple-element.292), kind=kLoop, calls=%fused_computation.14.clone.1 | loop fusion | bytes 24788992 | tf_op jit(solution)/shard_map/while/body/eval_jaxpr/slice | solution.py:31
  191.9 18.5 %add_add_fusion.2 = f32[1,2,128,2048]{3,2,1,0:T(8,128)S(1)} fusion(f32[1,2,178,2176]{3,2,1,0:T(8,128)} %get-tuple-element.240, s32[]{:T(128)S(6)} %select_n.298, s32[]{:T(128)S(6)} %select_n.300, s32[]{:T(128)S(6)} %select_n.301, s32[]{:T(128)S(6)} %select_n.302, f32[1,2,178,2176]{3,2,1,0:T(8,128)} %get-tuple-element.244, s32[]{:T(128)S(6)} %select_n.304, ...), kind=kLoop, calls=%fused_computation.clone.1 | loop fusion | flops 20447232 | bytes 35651712 | tf_op jit(solution)/shard_map/while/body/eval_jaxpr/add | solution.py:45
  210.4 1.2 fusion.14
  211.6 0.6 fusion.12
  212.2 0.6 fusion.13
  222.8 8.6 %fusion.11 = (f32[1,2,178,2176]{3,2,1,0:T(8,128)S(1)}, f32[1,2,178,2176]{3,2,1,0:T(8,128)}, f32[1,2,178,2176]{3,2,1,0:T(8,128)}, f32[1,2,178,2176]{3,2,1,0:T(8,128)}) fusion(f32[4,2,178,2176]{3,2,1,0:T(8,128)} %get-tuple-element.292), kind=kLoop, calls=%fused_computation.14.clone.1 | loop fusion | bytes 24788992 | tf_op jit(solution)/shard_map/while/body/eval_jaxpr/slice | solution.py:31
  231.3 18.8 %add_add_fusion.2 = f32[1,2,128,2048]{3,2,1,0:T(8,128)S(1)} fusion(f32[1,2,178,2176]{3,2,1,0:T(8,128)} %get-tuple-element.240, s32[]{:T(128)S(6)} %select_n.298, s32[]{:T(128)S(6)} %select_n.300, s32[]{:T(128)S(6)} %select_n.301, s32[]{:T(128)S(6)} %select_n.302, f32[1,2,178,2176]{3,2,1,0:T(8,128)} %get-tuple-element.244, s32[]{:T(128)S(6)} %select_n.304, ...), kind=kLoop, calls=%fused_computation.clone.1 | loop fusion | flops 20447232 | bytes 35651712 | tf_op jit(solution)/shard_map/while/body/eval_jaxpr/add | solution.py:45
  250.2 1.2 fusion.14
  251.4 0.6 fusion.12
  252.0 0.6 fusion.13
  262.5 8.6 %fusion.11 = (f32[1,2,178,2176]{3,2,1,0:T(8,128)S(1)}, f32[1,2,178,2176]{3,2,1,0:T(8,128)}, f32[1,2,178,2176]{3,2,1,0:T(8,128)}, f32[1,2,178,2176]{3,2,1,0:T(8,128)}) fusion(f32[4,2,178,2176]{3,2,1,0:T(8,128)} %get-tuple-element.292), kind=kLoop, calls=%fused_computation.14.clone.1 | loop fusion | bytes 24788992 | tf_op jit(solution)/shard_map/while/body/eval_jaxpr/slice | solution.py:31
  271.1 18.3 %add_add_fusion.2 = f32[1,2,128,2048]{3,2,1,0:T(8,128)S(1)} fusion(f32[1,2,178,2176]{3,2,1,0:T(8,128)} %get-tuple-element.240, s32[]{:T(128)S(6)} %select_n.298, s32[]{:T(128)S(6)} %select_n.300, s32[]{:T(128)S(6)} %select_n.301, s32[]{:T(128)S(6)} %select_n.302, f32[1,2,178,2176]{3,2,1,0:T(8,128)} %get-tuple-element.244, s32[]{:T(128)S(6)} %select_n.304, ...), kind=kLoop, calls=%fused_computation.clone.1 | loop fusion | flops 20447232 | bytes 35651712 | tf_op jit(solution)/shard_map/while/body/eval_jaxpr/add | solution.py:45
  289.4 1.2 fusion.14
  290.6 0.6 fusion.12
  291.2 0.6 fusion.13
  301.8 8.6 %fusion.11 = (f32[1,2,178,2176]{3,2,1,0:T(8,128)S(1)}, f32[1,2,178,2176]{3,2,1,0:T(8,128)}, f32[1,2,178,2176]{3,2,1,0:T(8,128)}, f32[1,2,178,2176]{3,2,1,0:T(8,128)}) fusion(f32[4,2,178,2176]{3,2,1,0:T(8,128)} %get-tuple-element.292), kind=kLoop, calls=%fused_computation.14.clone.1 | loop fusion | bytes 24788992 | tf_op jit(solution)/shard_map/while/body/eval_jaxpr/slice | solution.py:31
  310.4 18.9 %add_add_fusion.2 = f32[1,2,128,2048]{3,2,1,0:T(8,128)S(1)} fusion(f32[1,2,178,2176]{3,2,1,0:T(8,128)} %get-tuple-element.240, s32[]{:T(128)S(6)} %select_n.298, s32[]{:T(128)S(6)} %select_n.300, s32[]{:T(128)S(6)} %select_n.301, s32[]{:T(128)S(6)} %select_n.302, f32[1,2,178,2176]{3,2,1,0:T(8,128)} %get-tuple-element.244, s32[]{:T(128)S(6)} %select_n.304, ...), kind=kLoop, calls=%fused_computation.clone.1 | loop fusion | flops 20447232 | bytes 35651712 | tf_op jit(solution)/shard_map/while/body/eval_jaxpr/add | solution.py:45
  329.3 1.2 fusion.14
  330.5 0.6 fusion.12
  331.1 0.6 fusion.13
  341.7 8.6 %fusion.11 = (f32[1,2,178,2176]{3,2,1,0:T(8,128)S(1)}, f32[1,2,178,2176]{3,2,1,0:T(8,128)}, f32[1,2,178,2176]{3,2,1,0:T(8,128)}, f32[1,2,178,2176]{3,2,1,0:T(8,128)}) fusion(f32[4,2,178,2176]{3,2,1,0:T(8,128)} %get-tuple-element.292), kind=kLoop, calls=%fused_computation.14.clone.1 | loop fusion | bytes 24788992 | tf_op jit(solution)/shard_map/while/body/eval_jaxpr/slice | solution.py:31
  350.2 18.9 %add_add_fusion.2 = f32[1,2,128,2048]{3,2,1,0:T(8,128)S(1)} fusion(f32[1,2,178,2176]{3,2,1,0:T(8,128)} %get-tuple-element.240, s32[]{:T(128)S(6)} %select_n.298, s32[]{:T(128)S(6)} %select_n.300, s32[]{:T(128)S(6)} %select_n.301, s32[]{:T(128)S(6)} %select_n.302, f32[1,2,178,2176]{3,2,1,0:T(8,128)} %get-tuple-element.244, s32[]{:T(128)S(6)} %select_n.304, ...), kind=kLoop, calls=%fused_computation.clone.1 | loop fusion | flops 20447232 | bytes 35651712 | tf_op jit(solution)/shard_map/while/body/eval_jaxpr/add | solution.py:45
  369.2 1.2 fusion.14
  370.4 0.6 fusion.12
  371.0 0.6 fusion.13
  381.5 8.6 %fusion.11 = (f32[1,2,178,2176]{3,2,1,0:T(8,128)S(1)}, f32[1,2,178,2176]{3,2,1,0:T(8,128)}, f32[1,2,178,2176]{3,2,1,0:T(8,128)}, f32[1,2,178,2176]{3,2,1,0:T(8,128)}) fusion(f32[4,2,178,2176]{3,2,1,0:T(8,128)} %get-tuple-element.292), kind=kLoop, calls=%fused_computation.14.clone.1 | loop fusion | bytes 24788992 | tf_op jit(solution)/shard_map/while/body/eval_jaxpr/slice | solution.py:31
  390.1 18.9 %add_add_fusion.2 = f32[1,2,128,2048]{3,2,1,0:T(8,128)S(1)} fusion(f32[1,2,178,2176]{3,2,1,0:T(8,128)} %get-tuple-element.240, s32[]{:T(128)S(6)} %select_n.298, s32[]{:T(128)S(6)} %select_n.300, s32[]{:T(128)S(6)} %select_n.301, s32[]{:T(128)S(6)} %select_n.302, f32[1,2,178,2176]{3,2,1,0:T(8,128)} %get-tuple-element.244, s32[]{:T(128)S(6)} %select_n.304, ...), kind=kLoop, calls=%fused_computation.clone.1 | loop fusion | flops 20447232 | bytes 35651712 | tf_op jit(solution)/shard_map/while/body/eval_jaxpr/add | solution.py:45
  409.0 1.2 fusion.14
  410.3 0.6 fusion.12
  410.9 0.6 fusion.13
  421.4 8.6 %fusion.11 = (f32[1,2,178,2176]{3,2,1,0:T(8,128)S(1)}, f32[1,2,178,2176]{3,2,1,0:T(8,128)}, f32[1,2,178,2176]{3,2,1,0:T(8,128)}, f32[1,2,178,2176]{3,2,1,0:T(8,128)}) fusion(f32[4,2,178,2176]{3,2,1,0:T(8,128)} %get-tuple-element.292), kind=kLoop, calls=%fused_computation.14.clone.1 | loop fusion | bytes 24788992 | tf_op jit(solution)/shard_map/while/body/eval_jaxpr/slice | solution.py:31
  430.0 18.9 %add_add_fusion.2 = f32[1,2,128,2048]{3,2,1,0:T(8,128)S(1)} fusion(f32[1,2,178,2176]{3,2,1,0:T(8,128)} %get-tuple-element.240, s32[]{:T(128)S(6)} %select_n.298, s32[]{:T(128)S(6)} %select_n.300, s32[]{:T(128)S(6)} %select_n.301, s32[]{:T(128)S(6)} %select_n.302, f32[1,2,178,2176]{3,2,1,0:T(8,128)} %get-tuple-element.244, s32[]{:T(128)S(6)} %select_n.304, ...), kind=kLoop, calls=%fused_computation.clone.1 | loop fusion | flops 20447232 | bytes 35651712 | tf_op jit(solution)/shard_map/while/body/eval_jaxpr/add | solution.py:45
  448.9 1.2 fusion.14
  (21 shorter events, 1.0 us)
Async XLA Ops:
  6.5 31.8 %copy-start = (s32[32,2]{0,1:T(2,128)S(1)}, s32[32,2]{0,1:T(2,128)}, u32[]{:S(2)}) copy-start(s32[32,2]{0,1:T(2,128)} %param.10) | copy-start | bytes 772
  6.5 2.0 copy-start.1
  6.5 113.3 %all-gather.2.cloned.1.call-start = ((), (), s32[]{:S(2)}) async-start(), calls=%async_computation | async-start | bytes 15073280 | tf_op jit(solution)/shard_map/all_gather | solution.py:62
  8.9 27.2 %collective-permute-start = (f32[4,2,25,512]{3,2,1,0:T(8,128)S(1)}, f32[4,2,25,512]{3,2,1,0:T(8,128)S(1)}, u32[]{:S(2)}, u32[]{:S(2)}) collective-permute-start(f32[4,2,25,512]{3,2,1,0:T(8,128)S(1)} %get-tuple-element.197), channel_id=1, source_target_pairs={{0,4},{4,8},{8,12},{12,16},{16,20},{20,24},{24,28},{1,5},{5,9},{9,... | collective-permute-start | bytes 1228808 | tf_op jit(solution)/shard_map/ppermute | solution.py:14
  13.7 22.4 %collective-permute-start.1 = (f32[4,2,25,512]{3,2,1,0:T(8,128)S(1)}, f32[4,2,25,512]{3,2,1,0:T(8,128)S(1)}, u32[]{:S(2)}, u32[]{:S(2)}) collective-permute-start(f32[4,2,25,512]{3,2,1,0:T(8,128)S(1)} %get-tuple-element.198), channel_id=1, source_target_pairs={{4,0},{8,4},{12,8},{16,12},{20,16},{24,20},{28,24},{5,1},{9,5},{13... | collective-permute-start | bytes 1228808 | tf_op jit(solution)/shard_map/ppermute | solution.py:17
  38.4 93.8 %copy-start.2 = (s32[4]{0:T(128)S(1)}, s32[4]{0:T(128)}, u32[]{:S(2)}) copy-start(s32[4]{0:T(128)} %param.11) | copy-start | bytes 52
Sparse Core Ops, SparseCore 0:
  38.4 81.3 all-gather.1
where the time goes:
time: 458 us; the launch traced here: 457 us
  other arithmetic  164 us (36%)
  waiting for transfers between devices  102 us (22%)
  local copies, waits for them, and re-layouts  91.3 us (20%)
  loops' own time  79.5 us (17%)
  between operations  13.5 us (3%)
  starting transfers between devices  6.17 us (1%)
    add x8, other arithmetic, stack_maps(): total = total + ((1.0 - frac_row) * upper + frac_row * lower)  150 us
    all_gather x1, waiting for transfers between devices, body(): whole_rows = lax.all_gather(with_rim, 'vel', axis=3, tiled=True)  81.4 us
    another operation x1, loops' own time, body(): return lax.map(own_velocity, own_velocities)  79.5 us
    slice x8, local copies, waits for them, and re-layouts, stack_maps(): layer = padded[exposure]  68.5 us
    ppermute x1, waiting for transfers between devices, padded_2(): lax.ppermute(lax.slice_in_dim(block, block.shape[dim] - width, None, axis...  21.1 us
    pad x1, local copies, waits for them, and re-layouts, pad_right(): return jnp.pad(block, ((0, 0), (0, 0), (0, 0), (HALO, target - have)))  12.4 us
    dynamic_update_slice x8, other arithmetic, body(): return lax.map(own_velocity, own_velocities)  9.33 us
  transfers between devices with their start and end apart: 3, of which 2 were waited for; matrix products, arithmetic and copies ran while one was open for 0% of the time, Pallas kernels for 0%

commit v1 on v0

v1 whole, which is shorter than its diff:
```python
import functools

import jax
import jax.numpy as jnp
from jax import lax
from jax.experimental import pallas as pl
from jax.experimental.pallas import tpu as pltpu
from jax.sharding import PartitionSpec as P

REACH = 24
LANES = 128
MIB = 1024 * 1024


def keep_kernel(psi_ref, phi_ref, mask_ref, edges_ref, mid_ref, first_ref):
    exposures, rows, cols = psi_ref.shape
    for exposure in range(exposures):
        for tile in range(cols // LANES):
            columns = pl.ds(tile * LANES, LANES)
            keep = mask_ref[exposure, :, columns] == 0
            for layer, ref in enumerate((psi_ref, phi_ref)):
                kept = jnp.where(keep, ref[exposure, :, columns], 0.0)
                if exposure == 0:
                    first_ref[layer, tile] = kept
                else:
                    edges_ref[0, exposure - 1, layer, tile] = kept[:REACH]
                    mid_ref[exposure - 1, layer, tile] = kept[REACH : rows - REACH]
                    edges_ref[1, exposure - 1, layer, tile] = kept[rows - REACH :]


def keep(psi, phi, mask):
    exposures, rows, cols = psi.shape
    tiles = cols // LANES
    later = exposures - 1
    f32 = jnp.float32
    return pl.pallas_call(
        keep_kernel,
        out_shape=(
            jax.ShapeDtypeStruct((2, later, 2, tiles, REACH, LANES), f32),
            jax.ShapeDtypeStruct((later, 2, tiles, rows - 2 * REACH, LANES), f32),
            jax.ShapeDtypeStruct((2, tiles, rows, LANES), f32),
        ),
        compiler_params=pltpu.CompilerParams(vmem_limit_bytes=32 * MIB),
    )(psi, phi, mask)


def stack_kernel(pieces, tiles, later, rows, per_device, *refs):
    velocity_ref, offset_ref, owner_ref = refs[:3]
    piece_refs = refs[3 : 3 + 5 * pieces]
    out_ref, image, first, sems = refs[3 + 5 * pieces :]
    all_tiles = pieces * tiles
    step = pl.program_id(0)
    lane = lax.broadcasted_iota(jnp.int32, (8, LANES), 1)

    @pl.when(step == 0)
    def _():
        copies = []
        for piece in range(pieces):
            above, edges, mid, below, own_first = piece_refs[5 * piece : 5 * piece + 5]
            place = owner_ref[piece] * tiles
            moves = (
                (above, 0, REACH),
                (edges.at[0], REACH, REACH),
                (mid, 2 * REACH, rows - 2 * REACH),
                (edges.at[1], rows, REACH),
                (below, rows + REACH, REACH),
            )
            for source, start, count in moves:
                target = image.at[:, :, 0, pl.ds(1 + place, tiles), pl.ds(start, count), :]
                copies.append(pltpu.make_async_copy(source, target, sems.at[len(copies)]))
            target = first.at[:, pl.ds(place, tiles)]
            copies.append(pltpu.make_async_copy(own_first, target, sems.at[len(copies)]))
        for copy in copies:
            copy.start()
        depth = image.shape[4]
        blank = jnp.zeros((depth, LANES), jnp.float32)
        for exposure in range(later):
            for layer in range(2):
                image[exposure, layer, 0, 0] = blank
                for part in range(4):
                    image[exposure, layer, part, all_tiles + 1] = blank
                for tile in range(all_tiles):
                    image[exposure, layer, 0, tile + 1, rows + 2 * REACH :] = blank[rows + 2 * REACH :]
        for copy in copies:
            copy.wait()
        wide_lane = lax.broadcasted_iota(jnp.int32, (depth, LANES), 1)

        def interpolate(index, carry):
            exposure = index // (2 * (all_tiles + 1))
            layer = index // (all_tiles + 1) % 2
            tile = index % (all_tiles + 1)
            left = image[exposure, layer, 0, tile]
            right = image[exposure, layer, 0, tile + 1]
            moved = jnp.where(
                wide_lane < LANES - 1,
                pltpu.roll(left, LANES - 1, 1),
                pltpu.roll(right, LANES - 1, 1),
            )
            slope = moved - left
            for part in range(1, 4):
                image[exposure, layer, part, tile] = left + (0.25 * part) * slope
            return carry

        lax.fori_loop(0, later * 2 * (all_tiles + 1), interpolate, 0)

    index = owner_ref[0] * per_device + step
    plans = []
    for exposure in range(later):
        row_shift = velocity_ref[index, 0] * offset_ref[exposure + 1]
        col_shift = velocity_ref[index, 1] * offset_ref[exposure + 1]
        frac_row = jnp.broadcast_to((row_shift & 3).astype(jnp.float32) * 0.25, (8, LANES))
        start = LANES + (col_shift >> 2)
        inside = start & (LANES - 1)
        plans.append(
            (
                REACH + (row_shift >> 2),
                frac_row,
                col_shift & 3,
                start >> 7,
                (LANES - inside) & (LANES - 1),
                lane < LANES - inside,
            )
        )

    def row_group(group, carry):
        def turned(exposure, layer, tile):
            base, frac_row, part, skip, turn, _ = plans[exposure]
            upper = image[exposure, layer, part, skip + tile, pl.ds(base + 8 * group, 8), :]
            lower = image[exposure, layer, part, skip + tile, pl.ds(base + 8 * group + 1, 8), :]
            return pltpu.roll(upper + frac_row * (lower - upper), turn, 1)

        lanes = [(e, l) for e in range(later) for l in range(2)]
        held = {key: turned(*key, 0) for key in lanes}
        for tile in range(all_tiles):
            total = [first[layer, tile, pl.ds(pl.multiple_of(8 * group, 8), 8), :] for layer in range(2)]
            for key in lanes:
                following = turned(*key, tile + 1)
                total[key[1]] += jnp.where(plans[key[0]][5], held[key], following)
                held[key] = following
            out_ref[0, group, tile] = total[0] * lax.rsqrt(jnp.maximum(total[1], 1.0))
        return carry

    lax.fori_loop(0, rows // 8, row_group, 0)


def stack(velocities, time_offsets, owners, pieces, per_device):
    count = len(pieces)
    later, _, tiles, _, _ = pieces[0][2].shape
    rows = pieces[0][4].shape[2]
    all_tiles = count * tiles
    depth = rows + 2 * REACH + 8
    smem = pl.BlockSpec(memory_space=pltpu.SMEM)
    anywhere = pl.BlockSpec(memory_space=pl.ANY)
    flat = [array for piece in pieces for array in piece]
    out = pl.pallas_call(
        functools.partial(stack_kernel, count, tiles, later, rows, per_device),
        grid=(per_device,),
        out_shape=jax.ShapeDtypeStruct((per_device, rows // 8, all_tiles, 8, LANES), jnp.float32),
        in_specs=[smem] * 3 + [anywhere] * len(flat),
        out_specs=pl.BlockSpec((1, rows // 8, all_tiles, 8, LANES), lambda v: (v, 0, 0, 0, 0)),
        scratch_shapes=[
            pltpu.VMEM((later, 2, 4, all_tiles + 2, depth, LANES), jnp.float32),
            pltpu.VMEM((2, all_tiles, rows, LANES), jnp.float32),
            pltpu.SemaphoreType.DMA((6 * count,)),
        ],
        compiler_params=pltpu.CompilerParams(vmem_limit_bytes=56 * MIB),
    )(velocities, time_offsets, owners, *flat)
    return out.transpose(0, 1, 3, 2, 4).reshape(per_device, rows, all_tiles * LANES)


def after(value, *earlier):
    return lax.optimization_barrier((value, *earlier))[0]


def body(psi, phi, mask, velocities, time_offsets):
    count = lax.axis_size("vel")
    skies = lax.axis_size("sky")
    per_device = velocities.shape[0] // count
    me = lax.axis_index("vel")
    edges, mid, first = keep(psi, phi, mask)

    def swap(value, bits):
        return lax.ppermute(value, "vel", [(i, i ^ bits) for i in range(count)])

    def from_rows_above(value):
        return lax.ppermute(value, "sky", [(i, i + 1) for i in range(skies - 1)])

    def from_rows_below(value):
        return lax.ppermute(value, "sky", [(i + 1, i) for i in range(skies - 1)])

    far = [2 * k for k in range(1, count // 2)]
    far_edges = [edges] + [swap(edges, bits) for bits in far]
    far_mid = [mid] + [swap(after(mid, far_edges[-1]), bits) for bits in far]
    far_first = [first] + [swap(after(first, far_mid[-1]), bits) for bits in far]
    pieces, owners = [], []
    for k in range(count // 2):
        above = from_rows_above(far_edges[k][1])
        below = from_rows_below(far_edges[k][0])
        pieces.append((above, far_edges[k], far_mid[k], below, far_first[k]))
        owners.append(me ^ (2 * k))
    for k in range(count // 2):
        pieces.append(tuple(swap(array, 1) for array in pieces[k]))
        owners.append(me ^ (2 * k + 1))
    owners = jnp.stack(owners).astype(jnp.int32)
    return stack(velocities, time_offsets, owners, pieces, per_device)


def solution(mesh):
    return jax.shard_map(
        body,
        mesh=mesh,
        in_specs=(P(None, "sky", "vel"), P(None, "sky", "vel"), P(None, "sky", "vel"), P(), P()),
        out_specs=P("vel", "sky", None),
        check_vma=False,
    )
```

time: 458 us -> 113 us (0.25)
  other arithmetic: 164 us -> 0.58 us
  local copies, waits for them, and re-layouts: 91.3 us -> 7.64 us
  loops' own time: 79.5 us -> 0 us
  waiting for transfers between devices: 102 us -> 38.8 us
  Pallas kernels: 0 us -> 45.1 us
  starting transfers between devices: 6.17 us -> 20 us
  between operations: 13.5 us -> 0.19 us
    add x8 -> x0, other arithmetic: 150 us -> none  [stack_maps(): total = total + ((1.0 - frac_row) * upper + frac_row * lower)]
    all_gather x1 -> x0, waiting for transfers between devices: 81.4 us -> none  [body(): whole_rows = lax.all_gather(with_rim, 'vel', axis=3, tiled=True)]
    another operation x1 -> x0, loops' own time: 79.5 us -> none  [body(): return lax.map(own_velocity, own_velocities)]
    slice x24 -> x0, local copies, waits for them, and re-layouts: 78.3 us -> none  [the longest x8 68.5 us: stack_maps(): layer = padded[exposure]]
    pallas_call x0 -> x2, Pallas kernels: none -> 45.1 us  [the longest x1 44.9 us: stack(): pl.pallas_call(functools.partial(stack_kernel, count, tiles, later, rows,...]
    ppermute x2 -> x17, waiting for transfers between devices: 21.1 us -> 38.8 us  [the longest x13 19.6 us: swap(): return lax.ppermute(value, 'vel', [(i, i ^ bits) for i in range(count)])]
    ppermute x2 -> x17, starting transfers between devices: 6.17 us -> 20 us  [the longest x2 9.82 us: from_rows_above(): return lax.ppermute(value, 'sky', [(i, i + 1) for i in range(skies - 1)])]
    pad x1 -> x0, local copies, waits for them, and re-layouts: 12.4 us -> none  [pad_right(): return jnp.pad(block, ((0, 0), (0, 0), (0, 0), (HALO, target - have)))]
  transfers between devices with their start and end apart: 3 -> 17, of which waited for: 2 -> 7; matrix products, arithmetic and copies ran while one was open for 0% -> 2% of each run, Pallas kernels for 0% -> 0%
where the time goes in v1:
time: 113 us; the launch traced here: 112 us
  Pallas kernels  45.1 us (40%)
  waiting for transfers between devices  38.8 us (34%)
  starting transfers between devices  20 us (18%)
  local copies, waits for them, and re-layouts  7.64 us (7%)
    pallas_call x1, Pallas kernels, stack(): pl.pallas_call(functools.partial(stack_kernel, count, tiles, later, rows,...  44.9 us
    ppermute x13, waiting for transfers between devices, swap(): return lax.ppermute(value, 'vel', [(i, i ^ bits) for i in range(count)])  19.6 us
    ppermute x2, waiting for transfers between devices, from_rows_above(): return lax.ppermute(value, 'sky', [(i, i + 1) for i in range(skies - 1)])  11.1 us
    ppermute x2, starting transfers between devices, from_rows_above(): return lax.ppermute(value, 'sky', [(i, i + 1) for i in range(skies - 1)])  9.82 us
    ppermute x2, waiting for transfers between devices, from_rows_below(): return lax.ppermute(value, 'sky', [(i + 1, i) for i in range(skies - 1)])  8.16 us
    ppermute x13, starting transfers between devices, swap(): return lax.ppermute(value, 'vel', [(i, i ^ bits) for i in range(count)])  7.57 us
    unnamed x29, local copies, waits for them, and re-layouts  7.56 us
    ppermute x2, starting transfers between devices, from_rows_below(): return lax.ppermute(value, 'sky', [(i + 1, i) for i in range(skies - 1)])  2.58 us
  transfers between devices with their start and end apart: 17, of which 7 were waited for; matrix products, arithmetic and copies ran while one was open for 2% of the time, Pallas kernels for 0%

profile of v1, /device:TPU:0, one launch (start us, length us, event | category | flops | bytes accessed | tf_op | source)
XLA Modules:
  0.0 112.3 jit_solution(7113258421291993306)
XLA Ops:
  0.0 1.2 %copy-done.1 = f32[4,128,512]{2,1,0:T(8,128)S(1)} copy-done((f32[4,128,512]{2,1,0:T(8,128)S(1)}, f32[4,128,512]{2,1,0:T(8,128)}, u32[]{:S(2)}) %copy-start.1) | copy-done | bytes 1048600
  1.2 1.2 %copy-done.2 = f32[4,128,512]{2,1,0:T(8,128)S(1)} copy-done((f32[4,128,512]{2,1,0:T(8,128)S(1)}, f32[4,128,512]{2,1,0:T(8,128)}, u32[]{:S(2)}) %copy-start.2) | copy-done | bytes 1048600
  2.5 1.2 %copy-done.3 = s32[4,128,512]{2,1,0:T(8,128)S(1)} copy-done((s32[4,128,512]{2,1,0:T(8,128)S(1)}, s32[4,128,512]{2,1,0:T(8,128)}, u32[]{:S(2)}) %copy-start.3) | copy-done | bytes 1048600
  3.7 0.2 shard_map.55
  3.9 0.0 copy-start
  3.9 0.0 copy-start.4
  3.9 0.0 copy-start.5
  3.9 3.0 %collective-permute-start.2 = (f32[2,3,2,4,24,128]{5,4,3,2,1,0:T(8,128)S(1)}, f32[2,3,2,4,24,128]{5,4,3,2,1,0:T(8,128)S(1)}, u32[]{:S(2)}, u32[]{:S(2)}) collective-permute-start(f32[2,3,2,4,24,128]{5,4,3,2,1,0:T(8,128)S(1)} %get-tuple-element.10.refs_4_), channel_id=1, source_target_pairs={{0,2},{1,3},{2,0},{3,1},{4,6},{5,7},{6,4},{7,5},{8,10},{9,11},{10,... | collective-permute-start | bytes 1769480 | tf_op jit(solution)/shard_map/ppermute | solution.py:183
  7.0 13.3 %collective-permute-done.2.refs_9_ = f32[2,3,2,4,24,128]{5,4,3,2,1,0:T(8,128)S(1)} collective-permute-done((f32[2,3,2,4,24,128]{5,4,3,2,1,0:T(8,128)S(1)}, f32[2,3,2,4,24,128]{5,4,3,2,1,0:T(8,128)S(1)}, u32[]{:S(2)}, u32[]{:S(2)}) %collective-permute-start.2) | collective-permute-done | bytes 589856 | tf_op jit(solution)/shard_map/ppermute | solution.py:183
  20.3 1.7 %collective-permute-start.4 = (f32[3,2,4,80,128]{4,3,2,1,0:T(8,128)S(1)}, f32[3,2,4,80,128]{4,3,2,1,0:T(8,128)}, u32[]{:S(2)}, u32[]{:S(2)}) collective-permute-start(f32[3,2,4,80,128]{4,3,2,1,0:T(8,128)S(1)} %get-tuple-element.13.refs_5_), channel_id=1, source_target_pairs={{0,2},{1,3},{2,0},{3,1},{4,6},{5,7},{6,4},{7,5},{8,10},{9,11},{10,... | collective-permute-start | bytes 2949128 | tf_op jit(solution)/shard_map/ppermute | solution.py:183
  22.1 1.3 %collective-permute-start.1 = (f32[3,2,4,24,128]{4,3,2,1,0:T(8,128)S(1)}, f32[3,2,4,24,128]{4,3,2,1,0:T(8,128)S(1)}, u32[]{:S(2)}, u32[]{:S(2)}) collective-permute-start(f32[3,2,4,24,128]{4,3,2,1,0:T(8,128)S(1)} %get-tuple-element.17), channel_id=1, source_target_pairs={{4,0},{8,4},{12,8},{16,12},{20,16},{24,20},{28,24},{5,1},{9,5},{13... | collective-permute-start | bytes 884744 | tf_op jit(solution)/shard_map/ppermute | solution.py:189
  23.4 0.1 collective-permute-start.11
  23.5 4.6 %collective-permute-start = (f32[3,2,4,24,128]{4,3,2,1,0:T(8,128)S(1)}, f32[3,2,4,24,128]{4,3,2,1,0:T(8,128)S(1)}, u32[]{:S(2)}, u32[]{:S(2)}) collective-permute-start(f32[3,2,4,24,128]{4,3,2,1,0:T(8,128)S(1)} %get-tuple-element.18), channel_id=1, source_target_pairs={{0,4},{4,8},{8,12},{12,16},{16,20},{20,24},{24,28},{1,5},{5,9},{9,... | collective-permute-start | bytes 884744 | tf_op jit(solution)/shard_map/ppermute | solution.py:186
  28.0 3.5 %collective-permute-done.1.refs_6_ = f32[3,2,4,24,128]{4,3,2,1,0:T(8,128)S(1)} collective-permute-done((f32[3,2,4,24,128]{4,3,2,1,0:T(8,128)S(1)}, f32[3,2,4,24,128]{4,3,2,1,0:T(8,128)S(1)}, u32[]{:S(2)}, u32[]{:S(2)}) %collective-permute-start.1) | collective-permute-done | bytes 294944 | tf_op jit(solution)/shard_map/ppermute | solution.py:189
  31.6 0.0 collective-permute-start.10
  31.6 0.5 collective-permute-start.9
  32.1 5.7 %collective-permute-done.refs_3_ = f32[3,2,4,24,128]{4,3,2,1,0:T(8,128)S(1)} collective-permute-done((f32[3,2,4,24,128]{4,3,2,1,0:T(8,128)S(1)}, f32[3,2,4,24,128]{4,3,2,1,0:T(8,128)S(1)}, u32[]{:S(2)}, u32[]{:S(2)}) %collective-permute-start) | collective-permute-done | bytes 294944 | tf_op jit(solution)/shard_map/ppermute | solution.py:186
  37.8 0.0 collective-permute-start.8
  37.9 5.5 %collective-permute-done.4.refs_10_ = f32[3,2,4,80,128]{4,3,2,1,0:T(8,128)} collective-permute-done((f32[3,2,4,80,128]{4,3,2,1,0:T(8,128)S(1)}, f32[3,2,4,80,128]{4,3,2,1,0:T(8,128)}, u32[]{:S(2)}, u32[]{:S(2)}) %collective-permute-start.4) | collective-permute-done | bytes 983072 | tf_op jit(solution)/shard_map/ppermute | solution.py:183
  43.3 0.0 collective-permute-start.7
  43.3 0.0 collective-permute-done.11.refs_17_
  43.4 0.8 copy-done.9
  44.2 1.4 %collective-permute-start.6 = (f32[2,4,128,128]{3,2,1,0:T(8,128)S(1)}, f32[2,4,128,128]{3,2,1,0:T(8,128)}, u32[]{:S(2)}, u32[]{:S(2)}) collective-permute-start(f32[2,4,128,128]{3,2,1,0:T(8,128)S(1)} %get-tuple-element.14.refs_7_), channel_id=1, source_target_pairs={{0,2},{1,3},{2,0},{3,1},{4,6},{5,7},{6,4},{7,5},{8,10},{9,11},{10,... | collective-permute-start | bytes 1572872 | tf_op jit(solution)/shard_map/ppermute | solution.py:183
  45.6 0.0 collective-permute-done.10.refs_16_
  45.6 0.7 copy-done.12
  46.3 0.2 collective-permute-start.14
  46.6 0.0 collective-permute-done.7.refs_13_
  46.6 1.3 %collective-permute-start.5 = (f32[3,2,4,24,128]{4,3,2,1,0:T(8,128)S(1)}, f32[3,2,4,24,128]{4,3,2,1,0:T(8,128)}, u32[]{:S(2)}, u32[]{:S(2)}) collective-permute-start(f32[3,2,4,24,128]{4,3,2,1,0:T(8,128)S(1)} %get-tuple-element.15), channel_id=1, source_target_pairs={{4,0},{8,4},{12,8},{16,12},{20,16},{24,20},{28,24},{5,1},{9,5},{13... | collective-permute-start | bytes 884744 | tf_op jit(solution)/shard_map/ppermute | solution.py:189
  47.9 0.0 collective-permute-done.8.refs_14_
  47.9 5.3 %collective-permute-start.3 = (f32[3,2,4,24,128]{4,3,2,1,0:T(8,128)S(1)}, f32[3,2,4,24,128]{4,3,2,1,0:T(8,128)}, u32[]{:S(2)}, u32[]{:S(2)}) collective-permute-start(f32[3,2,4,24,128]{4,3,2,1,0:T(8,128)S(1)} %get-tuple-element.16), channel_id=1, source_target_pairs={{0,4},{4,8},{8,12},{12,16},{16,20},{20,24},{24,28},{1,5},{5,9},{9,... | collective-permute-start | bytes 884744 | tf_op jit(solution)/shard_map/ppermute | solution.py:186
  53.2 4.6 %collective-permute-done.5.refs_11_ = f32[3,2,4,24,128]{4,3,2,1,0:T(8,128)} collective-permute-done((f32[3,2,4,24,128]{4,3,2,1,0:T(8,128)S(1)}, f32[3,2,4,24,128]{4,3,2,1,0:T(8,128)}, u32[]{:S(2)}, u32[]{:S(2)}) %collective-permute-start.5) | collective-permute-done | bytes 294944 | tf_op jit(solution)/shard_map/ppermute | solution.py:189
  57.8 0.0 collective-permute-start.13
  57.8 0.8 collective-permute-done.6.refs_12_
  58.6 0.0 collective-permute-start.16
  58.6 5.3 %collective-permute-done.3.refs_8_ = f32[3,2,4,24,128]{4,3,2,1,0:T(8,128)} collective-permute-done((f32[3,2,4,24,128]{4,3,2,1,0:T(8,128)S(1)}, f32[3,2,4,24,128]{4,3,2,1,0:T(8,128)}, u32[]{:S(2)}, u32[]{:S(2)}) %collective-permute-start.3) | collective-permute-done | bytes 294944 | tf_op jit(solution)/shard_map/ppermute | solution.py:186
  63.9 0.0 collective-permute-start.15
  64.0 0.0 collective-permute-done.9.refs_15_
  64.0 1.0 copy-done.7
  64.9 0.5 collective-permute-start.12
  65.4 0.0 copy-done.13
  65.4 1.4 %copy.6.refs_0_ = s32[32,2]{1,0:T(8,128)} copy(s32[32,2]{0,1:T(2,128)} %param.8) | data formatting | bytes 512 | tf_op args[3]
  66.8 0.6 pad_add_fusion.refs_2_
  67.4 0.0 collective-permute-done.15.refs_21_
  67.4 0.0 collective-permute-done.12.refs_18_
  67.4 0.0 collective-permute-done.13.refs_19_
  67.4 0.0 collective-permute-done.14.refs_20_
  67.4 0.0 collective-permute-done.16.refs_22_
  67.4 44.9 %shard_map.56 = f32[8,16,16,8,128]{4,3,2,1,0:T(8,128)} custom-call(s32[32,2]{1,0:T(8,128)} %copy.6.refs_0_, s32[4]{0:T(128)} %refs_1_.1, s32[4]{0:T(128)} %pad_add_fusion.refs_2_, f32[3,2,4,24,128]{4,3,2,1,0:T(8,128)} %copy-done.11, f32[2,3,2,4,24,128]{5,4,3,2,1,0:T(8,128)} %copy-done, f32[3,2,4,80,128]{4,3,2,1,0:T(8,128)} %copy-done.4, ...), custom_call_target="tpu_custom_call" | custom-call | tf_op jit(solution)/shard_map/pallas_call | solution.py:155
  (20 shorter events, 0.1 us)
Async XLA Ops:
  0.0 1.2 %copy-start.1 = (f32[4,128,512]{2,1,0:T(8,128)S(1)}, f32[4,128,512]{2,1,0:T(8,128)}, u32[]{:S(2)}) copy-start(f32[4,128,512]{2,1,0:T(8,128)} %psi_ref.1) | copy-start | bytes 3145732
  1.2 1.2 %copy-start.2 = (f32[4,128,512]{2,1,0:T(8,128)S(1)}, f32[4,128,512]{2,1,0:T(8,128)}, u32[]{:S(2)}) copy-start(f32[4,128,512]{2,1,0:T(8,128)} %phi_ref.1) | copy-start | bytes 3145732
  2.5 1.2 %copy-start.3 = (s32[4,128,512]{2,1,0:T(8,128)S(1)}, s32[4,128,512]{2,1,0:T(8,128)}, u32[]{:S(2)}) copy-start(s32[4,128,512]{2,1,0:T(8,128)} %mask_ref.1) | copy-start | bytes 3145732
  3.9 63.5 %copy-start = (f32[2,3,2,4,24,128]{5,4,3,2,1,0:T(8,128)}, f32[2,3,2,4,24,128]{5,4,3,2,1,0:T(8,128)S(1)}, u32[]{:S(2)}) copy-start(f32[2,3,2,4,24,128]{5,4,3,2,1,0:T(8,128)S(1)} %get-tuple-element.10.refs_4_) | copy-start | bytes 1769476
  3.9 63.5 %copy-start.4 = (f32[3,2,4,80,128]{4,3,2,1,0:T(8,128)}, f32[3,2,4,80,128]{4,3,2,1,0:T(8,128)S(1)}, u32[]{:S(2)}) copy-start(f32[3,2,4,80,128]{4,3,2,1,0:T(8,128)S(1)} %get-tuple-element.13.refs_5_) | copy-start | bytes 2949124
  3.9 63.5 %copy-start.5 = (f32[2,4,128,128]{3,2,1,0:T(8,128)}, f32[2,4,128,128]{3,2,1,0:T(8,128)S(1)}, u32[]{:S(2)}) copy-start(f32[2,4,128,128]{3,2,1,0:T(8,128)S(1)} %get-tuple-element.14.refs_7_) | copy-start | bytes 1572868
  3.9 16.4 %collective-permute-start.2 = (f32[2,3,2,4,24,128]{5,4,3,2,1,0:T(8,128)S(1)}, f32[2,3,2,4,24,128]{5,4,3,2,1,0:T(8,128)S(1)}, u32[]{:S(2)}, u32[]{:S(2)}) collective-permute-start(f32[2,3,2,4,24,128]{5,4,3,2,1,0:T(8,128)S(1)} %get-tuple-element.10.refs_4_), channel_id=1, source_target_pairs={{0,2},{1,3},{2,0},{3,1},{4,6},{5,7},{6,4},{7,5},{8,10},{9,11},{10,... | collective-permute-start | bytes 1769480 | tf_op jit(solution)/shard_map/ppermute | solution.py:183
  20.3 47.1 %copy-start.6 = (f32[2,3,2,4,24,128]{5,4,3,2,1,0:T(8,128)}, f32[2,3,2,4,24,128]{5,4,3,2,1,0:T(8,128)S(1)}, u32[]{:S(2)}) copy-start(f32[2,3,2,4,24,128]{5,4,3,2,1,0:T(8,128)S(1)} %collective-permute-done.2.refs_9_) | copy-start | bytes 1769476
  20.3 23.0 %collective-permute-start.4 = (f32[3,2,4,80,128]{4,3,2,1,0:T(8,128)S(1)}, f32[3,2,4,80,128]{4,3,2,1,0:T(8,128)}, u32[]{:S(2)}, u32[]{:S(2)}) collective-permute-start(f32[3,2,4,80,128]{4,3,2,1,0:T(8,128)S(1)} %get-tuple-element.13.refs_5_), channel_id=1, source_target_pairs={{0,2},{1,3},{2,0},{3,1},{4,6},{5,7},{6,4},{7,5},{8,10},{9,11},{10,... | collective-permute-start | bytes 2949128 | tf_op jit(solution)/shard_map/ppermute | solution.py:183
  22.1 9.5 %collective-permute-start.1 = (f32[3,2,4,24,128]{4,3,2,1,0:T(8,128)S(1)}, f32[3,2,4,24,128]{4,3,2,1,0:T(8,128)S(1)}, u32[]{:S(2)}, u32[]{:S(2)}) collective-permute-start(f32[3,2,4,24,128]{4,3,2,1,0:T(8,128)S(1)} %get-tuple-element.17), channel_id=1, source_target_pairs={{4,0},{8,4},{12,8},{16,12},{20,16},{24,20},{28,24},{5,1},{9,5},{13... | collective-permute-start | bytes 884744 | tf_op jit(solution)/shard_map/ppermute | solution.py:189
  23.4 20.0 %collective-permute-start.11 = (f32[2,4,128,128]{3,2,1,0:T(8,128)S(1)}, f32[2,4,128,128]{3,2,1,0:T(8,128)S(1)}, u32[]{:S(2)}, u32[]{:S(2)}) collective-permute-start(f32[2,4,128,128]{3,2,1,0:T(8,128)S(1)} %get-tuple-element.14.refs_7_), channel_id=1, source_target_pairs={{0,1},{1,0},{2,3},{3,2},{4,5},{5,4},{6,7},{7,6},{8,9},{9,8},{10,11... | collective-permute-start | bytes 1572872 | tf_op jit(solution)/shard_map/ppermute | solution.py:183
  23.5 14.4 %collective-permute-start = (f32[3,2,4,24,128]{4,3,2,1,0:T(8,128)S(1)}, f32[3,2,4,24,128]{4,3,2,1,0:T(8,128)S(1)}, u32[]{:S(2)}, u32[]{:S(2)}) collective-permute-start(f32[3,2,4,24,128]{4,3,2,1,0:T(8,128)S(1)} %get-tuple-element.18), channel_id=1, source_target_pairs={{0,4},{4,8},{8,12},{12,16},{16,20},{20,24},{24,28},{1,5},{5,9},{9,... | collective-permute-start | bytes 884744 | tf_op jit(solution)/shard_map/ppermute | solution.py:186
  31.6 14.0 %copy-start.10 = (f32[3,2,4,24,128]{4,3,2,1,0:T(8,128)}, f32[3,2,4,24,128]{4,3,2,1,0:T(8,128)S(1)}, u32[]{:S(2)}) copy-start(f32[3,2,4,24,128]{4,3,2,1,0:T(8,128)S(1)} %collective-permute-done.1.refs_6_) | copy-start | bytes 884740
  31.6 14.0 %collective-permute-start.10 = (f32[3,2,4,24,128]{4,3,2,1,0:T(8,128)S(1)}, f32[3,2,4,24,128]{4,3,2,1,0:T(8,128)S(1)}, u32[]{:S(2)}, u32[]{:S(2)}) collective-permute-start(f32[3,2,4,24,128]{4,3,2,1,0:T(8,128)S(1)} %collective-permute-done.1.refs_6_), channel_id=1, source_target_pairs={{0,1},{1,0},{2,3},{3,2},{4,5},{5,4},{6,7},{7,6},{8,9},{9,8},{10,11... | collective-permute-start | bytes 884744 | tf_op jit(solution)/shard_map/ppermute | solution.py:183
  31.6 32.4 %collective-permute-start.9 = (f32[3,2,4,80,128]{4,3,2,1,0:T(8,128)S(1)}, f32[3,2,4,80,128]{4,3,2,1,0:T(8,128)S(1)}, u32[]{:S(2)}, u32[]{:S(2)}) collective-permute-start(f32[3,2,4,80,128]{4,3,2,1,0:T(8,128)S(1)} %get-tuple-element.13.refs_5_), channel_id=1, source_target_pairs={{0,1},{1,0},{2,3},{3,2},{4,5},{5,4},{6,7},{7,6},{8,9},{9,8},{10,11... | collective-permute-start | bytes 2949128 | tf_op jit(solution)/shard_map/ppermute | solution.py:183
  37.8 27.6 %copy-start.11 = (f32[3,2,4,24,128]{4,3,2,1,0:T(8,128)}, f32[3,2,4,24,128]{4,3,2,1,0:T(8,128)S(1)}, u32[]{:S(2)}) copy-start(f32[3,2,4,24,128]{4,3,2,1,0:T(8,128)S(1)} %collective-permute-done.refs_3_) | copy-start | bytes 884740
  37.8 10.1 %collective-permute-start.8 = (f32[2,3,2,4,24,128]{5,4,3,2,1,0:T(8,128)S(1)}, f32[2,3,2,4,24,128]{5,4,3,2,1,0:T(8,128)S(1)}, u32[]{:S(2)}, u32[]{:S(2)}) collective-permute-start(f32[2,3,2,4,24,128]{5,4,3,2,1,0:T(8,128)S(1)} %get-tuple-element.10.refs_4_), channel_id=1, source_target_pairs={{0,1},{1,0},{2,3},{3,2},{4,5},{5,4},{6,7},{7,6},{8,9},{9,8},{10,11... | collective-permute-start | bytes 1769480 | tf_op jit(solution)/shard_map/ppermute | solution.py:183
  43.3 3.3 %collective-permute-start.7 = (f32[3,2,4,24,128]{4,3,2,1,0:T(8,128)S(1)}, f32[3,2,4,24,128]{4,3,2,1,0:T(8,128)S(1)}, u32[]{:S(2)}, u32[]{:S(2)}) collective-permute-start(f32[3,2,4,24,128]{4,3,2,1,0:T(8,128)S(1)} %collective-permute-done.refs_3_), channel_id=1, source_target_pairs={{0,1},{1,0},{2,3},{3,2},{4,5},{5,4},{6,7},{7,6},{8,9},{9,8},{10,11... | collective-permute-start | bytes 884744 | tf_op jit(solution)/shard_map/ppermute | solution.py:183
  43.4 0.8 copy-start.9
  44.2 14.4 %collective-permute-start.6 = (f32[2,4,128,128]{3,2,1,0:T(8,128)S(1)}, f32[2,4,128,128]{3,2,1,0:T(8,128)}, u32[]{:S(2)}, u32[]{:S(2)}) collective-permute-start(f32[2,4,128,128]{3,2,1,0:T(8,128)S(1)} %get-tuple-element.14.refs_7_), channel_id=1, source_target_pairs={{0,2},{1,3},{2,0},{3,1},{4,6},{5,7},{6,4},{7,5},{8,10},{9,11},{10,... | collective-permute-start | bytes 1572872 | tf_op jit(solution)/shard_map/ppermute | solution.py:183
  45.6 0.7 copy-start.12
  46.3 21.0 %collective-permute-start.14 = (f32[3,2,4,80,128]{4,3,2,1,0:T(8,128)}, f32[3,2,4,80,128]{4,3,2,1,0:T(8,128)}, u32[]{:S(2)}, u32[]{:S(2)}) collective-permute-start(f32[3,2,4,80,128]{4,3,2,1,0:T(8,128)} %collective-permute-done.4.refs_10_), channel_id=1, source_target_pairs={{0,1},{1,0},{2,3},{3,2},{4,5},{5,4},{6,7},{7,6},{8,9},{9,8},{10,11... | collective-permute-start | bytes 2949128 | tf_op jit(solution)/shard_map/ppermute | solution.py:183
  46.6 18.8 %copy-start.13 = (f32[3,2,4,24,128]{4,3,2,1,0:T(8,128)}, f32[3,2,4,24,128]{4,3,2,1,0:T(8,128)S(1)}, u32[]{:S(2)}) copy-start(f32[3,2,4,24,128]{4,3,2,1,0:T(8,128)S(1)} %collective-permute-done.7.refs_13_) | copy-start | bytes 884740
  46.6 11.2 %collective-permute-start.5 = (f32[3,2,4,24,128]{4,3,2,1,0:T(8,128)S(1)}, f32[3,2,4,24,128]{4,3,2,1,0:T(8,128)}, u32[]{:S(2)}, u32[]{:S(2)}) collective-permute-start(f32[3,2,4,24,128]{4,3,2,1,0:T(8,128)S(1)} %get-tuple-element.15), channel_id=1, source_target_pairs={{4,0},{8,4},{12,8},{16,12},{20,16},{24,20},{28,24},{5,1},{9,5},{13... | collective-permute-start | bytes 884744 | tf_op jit(solution)/shard_map/ppermute | solution.py:189
  47.9 19.5 %copy-start.8 = (f32[2,3,2,4,24,128]{5,4,3,2,1,0:T(8,128)}, f32[2,3,2,4,24,128]{5,4,3,2,1,0:T(8,128)S(1)}, u32[]{:S(2)}) copy-start(f32[2,3,2,4,24,128]{5,4,3,2,1,0:T(8,128)S(1)} %collective-permute-done.8.refs_14_) | copy-start | bytes 1769476
  47.9 16.0 %collective-permute-start.3 = (f32[3,2,4,24,128]{4,3,2,1,0:T(8,128)S(1)}, f32[3,2,4,24,128]{4,3,2,1,0:T(8,128)}, u32[]{:S(2)}, u32[]{:S(2)}) collective-permute-start(f32[3,2,4,24,128]{4,3,2,1,0:T(8,128)S(1)} %get-tuple-element.16), channel_id=1, source_target_pairs={{0,4},{4,8},{8,12},{12,16},{16,20},{20,24},{24,28},{1,5},{5,9},{9,... | collective-permute-start | bytes 884744 | tf_op jit(solution)/shard_map/ppermute | solution.py:186
  57.8 9.5 %collective-permute-start.13 = (f32[2,3,2,4,24,128]{5,4,3,2,1,0:T(8,128)S(1)}, f32[2,3,2,4,24,128]{5,4,3,2,1,0:T(8,128)}, u32[]{:S(2)}, u32[]{:S(2)}) collective-permute-start(f32[2,3,2,4,24,128]{5,4,3,2,1,0:T(8,128)S(1)} %collective-permute-done.2.refs_9_), channel_id=1, source_target_pairs={{0,1},{1,0},{2,3},{3,2},{4,5},{5,4},{6,7},{7,6},{8,9},{9,8},{10,11... | collective-permute-start | bytes 1769480 | tf_op jit(solution)/shard_map/ppermute | solution.py:183
  58.6 8.8 %collective-permute-start.16 = (f32[2,4,128,128]{3,2,1,0:T(8,128)}, f32[2,4,128,128]{3,2,1,0:T(8,128)}, u32[]{:S(2)}, u32[]{:S(2)}) collective-permute-start(f32[2,4,128,128]{3,2,1,0:T(8,128)} %collective-permute-done.6.refs_12_), channel_id=1, source_target_pairs={{0,1},{1,0},{2,3},{3,2},{4,5},{5,4},{6,7},{7,6},{8,9},{9,8},{10,11... | collective-permute-start | bytes 1572872 | tf_op jit(solution)/shard_map/ppermute | solution.py:183
  63.9 3.4 %collective-permute-start.15 = (f32[3,2,4,24,128]{4,3,2,1,0:T(8,128)}, f32[3,2,4,24,128]{4,3,2,1,0:T(8,128)}, u32[]{:S(2)}, u32[]{:S(2)}) collective-permute-start(f32[3,2,4,24,128]{4,3,2,1,0:T(8,128)} %collective-permute-done.5.refs_11_), channel_id=1, source_target_pairs={{0,1},{1,0},{2,3},{3,2},{4,5},{5,4},{6,7},{7,6},{8,9},{9,8},{10,11... | collective-permute-start | bytes 884744 | tf_op jit(solution)/shard_map/ppermute | solution.py:183
  64.0 1.0 copy-start.7
  64.9 2.4 %collective-permute-start.12 = (f32[3,2,4,24,128]{4,3,2,1,0:T(8,128)}, f32[3,2,4,24,128]{4,3,2,1,0:T(8,128)}, u32[]{:S(2)}, u32[]{:S(2)}) collective-permute-start(f32[3,2,4,24,128]{4,3,2,1,0:T(8,128)} %collective-permute-done.3.refs_8_), channel_id=1, source_target_pairs={{0,1},{1,0},{2,3},{3,2},{4,5},{5,4},{6,7},{7,6},{8,9},{9,8},{10,11... | collective-permute-start | bytes 884744 | tf_op jit(solution)/shard_map/ppermute | solution.py:183

commit v2 on v1

v2 whole, which is shorter than its diff:
```python
import functools

import jax
import jax.numpy as jnp
from jax import lax
from jax.experimental import pallas as pl
from jax.experimental.pallas import tpu as pltpu
from jax.sharding import PartitionSpec as P

REACH = 24
LANES = 128
MIB = 1024 * 1024


def keep_kernel(psi_ref, phi_ref, mask_ref, top_ref, bottom_ref, mid_ref, last_ref, first_ref):
    exposures, rows, cols = psi_ref.shape
    for exposure in range(exposures):
        for tile in range(cols // LANES):
            columns = pl.ds(tile * LANES, LANES)
            keep = mask_ref[exposure, :, columns] == 0
            for layer, ref in enumerate((psi_ref, phi_ref)):
                kept = jnp.where(keep, ref[exposure, :, columns], 0.0)
                if exposure == 0:
                    first_ref[layer, tile] = kept
                    continue
                top_ref[exposure - 1, layer, tile] = kept[:REACH]
                bottom_ref[exposure - 1, layer, tile] = kept[rows - REACH :]
                middle = kept[REACH : rows - REACH]
                if exposure == exposures - 1:
                    last_ref[0, layer, tile] = middle
                else:
                    mid_ref[exposure - 1, layer, tile] = middle


def keep(psi, phi, mask):
    exposures, rows, cols = psi.shape
    tiles = cols // LANES
    later = exposures - 1
    shapes = [(later, 2, tiles, REACH, LANES)] * 2 + [
        (later - 1, 2, tiles, rows - 2 * REACH, LANES),
        (1, 2, tiles, rows - 2 * REACH, LANES),
        (2, tiles, rows, LANES),
    ]
    return pl.pallas_call(
        keep_kernel,
        out_shape=tuple(jax.ShapeDtypeStruct(shape, jnp.float32) for shape in shapes),
        compiler_params=pltpu.CompilerParams(vmem_limit_bytes=32 * MIB),
    )(psi, phi, mask)


def stack_kernel(pieces, tiles, begin, later, rows, per_device, final, *refs):
    velocity_ref, offset_ref, owner_ref = refs[:3]
    each = 6 if final else 5
    piece_refs = refs[3 : 3 + each * pieces]
    rest = refs[3 + each * pieces :]
    if final:
        sum_ref, out_ref, image, sems, first = rest
    else:
        out_ref, image, sems = rest
    all_tiles = pieces * tiles
    step = pl.program_id(0)
    lane = lax.broadcasted_iota(jnp.int32, (8, LANES), 1)

    @pl.when(step == 0)
    def _():
        copies = []
        for piece in range(pieces):
            above, top, mid, bottom, below = piece_refs[each * piece : each * piece + 5]
            place = owner_ref[piece] * tiles
            mine = pl.ds(begin, later)
            moves = (
                (above.at[mine], 0, REACH),
                (top.at[mine], REACH, REACH),
                (mid, 2 * REACH, rows - 2 * REACH),
                (bottom.at[mine], rows, REACH),
                (below.at[mine], rows + REACH, REACH),
            )
            for source, start, count in moves:
                target = image.at[:, :, 0, pl.ds(1 + place, tiles), pl.ds(start, count), :]
                copies.append(pltpu.make_async_copy(source, target, sems.at[len(copies)]))
            if final:
                target = first.at[:, pl.ds(place, tiles)]
                source = piece_refs[each * piece + 5]
                copies.append(pltpu.make_async_copy(source, target, sems.at[len(copies)]))
        for copy in copies:
            copy.start()
        depth = image.shape[4]
        blank = jnp.zeros((depth, LANES), jnp.float32)
        for exposure in range(later):
            for layer in range(2):
                image[exposure, layer, 0, 0] = blank
                for part in range(4):
                    image[exposure, layer, part, all_tiles + 1] = blank
                for tile in range(all_tiles):
                    image[exposure, layer, 0, tile + 1, rows + 2 * REACH :] = blank[rows + 2 * REACH :]
        for copy in copies:
            copy.wait()
        groups = depth // 8

        def interpolate(index, carry):
            exposure = index // (2 * groups)
            layer = index // groups % 2
            here = pl.ds(pl.multiple_of(index % groups * 8, 8), 8)
            left = image[exposure, layer, 0, 0, here, :]
            left_moved = pltpu.roll(left, LANES - 1, 1)
            for tile in range(all_tiles + 1):
                right = image[exposure, layer, 0, tile + 1, here, :]
                right_moved = pltpu.roll(right, LANES - 1, 1)
                slope = jnp.where(lane < LANES - 1, left_moved, right_moved) - left
                for part in range(1, 4):
                    image[exposure, layer, part, tile, here, :] = left + (0.25 * part) * slope
                left, left_moved = right, right_moved
            return carry

        lax.fori_loop(0, later * 2 * groups, interpolate, 0)

    index = owner_ref[0] * per_device + step
    plans = []
    for exposure in range(later):
        offset = offset_ref[begin + exposure + 1]
        row_shift = velocity_ref[index, 0] * offset
        col_shift = velocity_ref[index, 1] * offset
        frac_row = jnp.broadcast_to((row_shift & 3).astype(jnp.float32) * 0.25, (8, LANES))
        start = LANES + (col_shift >> 2)
        inside = start & (LANES - 1)
        plans.append(
            (
                REACH + (row_shift >> 2),
                frac_row,
                col_shift & 3,
                start >> 7,
                (LANES - inside) & (LANES - 1),
                lane < LANES - inside,
            )
        )

    def row_group(group, carry):
        def turned(exposure, layer, tile):
            base, frac_row, part, skip, turn, _ = plans[exposure]
            upper = image[exposure, layer, part, skip + tile, pl.ds(base + 8 * group, 8), :]
            lower = image[exposure, layer, part, skip + tile, pl.ds(base + 8 * group + 1, 8), :]
            return pltpu.roll(upper + frac_row * (lower - upper), turn, 1)

        held = {(e, l): turned(e, l, 0) for e in range(later) for l in range(2)}
        here = pl.ds(pl.multiple_of(8 * group, 8), 8)
        for tile in range(all_tiles):
            total = []
            for layer in range(2):
                terms = []
                if final:
                    terms = [first[layer, tile, here, :], sum_ref[0, layer, group, tile]]
                for exposure in range(later):
                    following = turned(exposure, layer, tile + 1)
                    terms.append(jnp.where(plans[exposure][5], held[exposure, layer], following))
                    held[exposure, layer] = following
                total.append(functools.reduce(jnp.add, terms))
            if final:
                out_ref[0, group, tile] = total[0] * lax.rsqrt(jnp.maximum(total[1], 1.0))
            else:
                out_ref[0, 0, group, tile] = total[0]
                out_ref[0, 1, group, tile] = total[1]
        return carry

    lax.fori_loop(0, rows // 8, row_group, 0)


def stack(velocities, time_offsets, owners, pieces, begin, rows, per_device, sums=None):
    final = sums is not None
    count = len(pieces)
    later, _, tiles, _, _ = pieces[0][2].shape
    all_tiles = count * tiles
    depth = rows + 2 * REACH + 8
    smem = pl.BlockSpec(memory_space=pltpu.SMEM)
    anywhere = pl.BlockSpec(memory_space=pl.ANY)
    block = (rows // 8, all_tiles, 8, LANES)
    sum_shape = (per_device, 2) + block
    out_shape = (per_device,) + block if final else sum_shape
    sum_spec = pl.BlockSpec((1, 2) + block, lambda v: (v, 0, 0, 0, 0, 0))
    out_spec = pl.BlockSpec((1,) + block, lambda v: (v, 0, 0, 0, 0)) if final else sum_spec
    flat = [array for piece in pieces for array in piece]
    scratch = [
        pltpu.VMEM((later, 2, 4, all_tiles + 2, depth, LANES), jnp.float32),
        pltpu.SemaphoreType.DMA((6 * count,)),
    ]
    if final:
        scratch.append(pltpu.VMEM((2, all_tiles, rows, LANES), jnp.float32))
    return pl.pallas_call(
        functools.partial(stack_kernel, count, tiles, begin, later, rows, per_device, final),
        grid=(per_device,),
        out_shape=jax.ShapeDtypeStruct(out_shape, jnp.float32),
        in_specs=[smem] * 3 + [anywhere] * len(flat) + ([sum_spec] if final else []),
        out_specs=out_spec,
        scratch_shapes=scratch,
        compiler_params=pltpu.CompilerParams(vmem_limit_bytes=44 * MIB),
        cost_estimate=pl.CostEstimate(
            flops=later * 8_000_000_000, bytes_accessed=later * 16 * MIB, transcendentals=0
        ),
    )(velocities, time_offsets, owners, *flat, *([sums] if final else []))


def after(value, *earlier):
    return lax.optimization_barrier((value, *earlier))[0]


def body(psi, phi, mask, velocities, time_offsets):
    count = lax.axis_size("vel")
    skies = lax.axis_size("sky")
    rows = psi.shape[1]
    later = psi.shape[0] - 1
    per_device = velocities.shape[0] // count
    me = lax.axis_index("vel")
    top, bottom, mid, last, first = keep(psi, phi, mask)

    def swap(value, bits):
        return lax.ppermute(value, "vel", [(i, i ^ bits) for i in range(count)])

    def from_rows_above(value):
        return lax.ppermute(value, "sky", [(i, i + 1) for i in range(skies - 1)])

    def from_rows_below(value):
        return lax.ppermute(value, "sky", [(i + 1, i) for i in range(skies - 1)])

    far = [2 * k for k in range(1, count // 2)]

    def gathered(value, *earlier):
        return [value] + [swap(after(value, *earlier), bits) for bits in far]

    tops = gathered(top)
    bottoms = gathered(bottom)
    mids = gathered(mid, tops[-1], bottoms[-1])
    lasts = gathered(last, mids[-1])
    firsts = gathered(first, lasts[-1])
    aboves = [from_rows_above(value) for value in bottoms]
    belows = [from_rows_below(value) for value in tops]
    owners = [me ^ (2 * k) for k in range(count // 2)] + [me ^ (2 * k + 1) for k in range(count // 2)]
    owners = jnp.stack(owners).astype(jnp.int32)

    def both_cores(arrays):
        return arrays + [swap(value, 1) for value in arrays]

    aboves, tops, bottoms, belows = map(both_cores, (aboves, tops, bottoms, belows))
    pieces = list(zip(aboves, tops, both_cores(mids), bottoms, belows))
    sums = stack(velocities, time_offsets, owners, pieces, 0, rows, per_device)
    firsts = [first] + [after(value, sums) for value in firsts[1:]]
    pieces = list(zip(aboves, tops, both_cores(lasts), bottoms, belows, both_cores(firsts)))
    out = stack(velocities, time_offsets, owners, pieces, later - 1, rows, per_device, sums)
    return out.transpose(0, 1, 3, 2, 4).reshape(per_device, rows, -1)


def solution(mesh):
    return jax.shard_map(
        body,
        mesh=mesh,
        in_specs=(P(None, "sky", "vel"), P(None, "sky", "vel"), P(None, "sky", "vel"), P(), P()),
        out_specs=P("vel", "sky", None),
        check_vma=False,
    )
```

time: 113 us -> 130 us (1.15)
  Pallas kernels: 45.1 us -> 60.1 us
  local copies, waits for them, and re-layouts: 7.64 us -> 10.1 us
    pallas_call x2 -> x3, Pallas kernels: 45.1 us -> 60.1 us  [the longest x2 59.1 us: stack(): pl.pallas_call(functools.partial(stack_kernel, count, tiles, begin, later...]
    ppermute x13 -> x19, waiting for transfers between devices: 19.6 us -> 15.4 us  [swap(): return lax.ppermute(value, 'vel', [(i, i ^ bits) for i in range(count)])]
    ppermute x2, waiting for transfers between devices: 11.1 us -> 15.1 us  [from_rows_above(): return lax.ppermute(value, 'sky', [(i, i + 1) for i in range(skies - 1)])]
    unnamed x29 -> x27, local copies, waits for them, and re-layouts: 7.56 us -> 10.1 us
    ppermute x13 -> x19, starting transfers between devices: 7.57 us -> 9.24 us  [swap(): return lax.ppermute(value, 'vel', [(i, i ^ bits) for i in range(count)])]
  transfers between devices with their start and end apart: 17 -> 23, of which waited for: 7 -> 8; matrix products, arithmetic and copies ran while one was open for 2% -> 1% of each run, Pallas kernels for 0% -> 27%
where the time goes in v2:
time: 130 us
  Pallas kernels  60.1 us (46%)
  waiting for transfers between devices  38.6 us (30%)
  starting transfers between devices  20.5 us (16%)
  local copies, waits for them, and re-layouts  10.1 us (8%)
    pallas_call x2, Pallas kernels, stack(): pl.pallas_call(functools.partial(stack_kernel, count, tiles, begin, later...  59.1 us
    ppermute x19, waiting for transfers between devices, swap(): return lax.ppermute(value, 'vel', [(i, i ^ bits) for i in range(count)])  15.4 us
    ppermute x2, waiting for transfers between devices, from_rows_above(): return lax.ppermute(value, 'sky', [(i, i + 1) for i in range(skies - 1)])  15.1 us
    unnamed x27, local copies, waits for them, and re-layouts  10.1 us
    ppermute x19, starting transfers between devices, swap(): return lax.ppermute(value, 'vel', [(i, i ^ bits) for i in range(count)])  9.24 us
    ppermute x2, starting transfers between devices, from_rows_above(): return lax.ppermute(value, 'sky', [(i, i + 1) for i in range(skies - 1)])  8.68 us
    ppermute x2, waiting for transfers between devices, from_rows_below(): return lax.ppermute(value, 'sky', [(i + 1, i) for i in range(skies - 1)])  8.19 us
  transfers between devices with their start and end apart: 23, of which 8 were waited for; matrix products, arithmetic and copies ran while one was open for 1% of the time, Pallas kernels for 27%

profile of v2, /device:TPU:0, one launch (start us, length us, event | category | flops | bytes accessed | tf_op | source)
XLA Modules:
  0.0 129.5 jit_solution(14436758518691339569)
XLA Ops:
  0.0 1.2 copy-done
  1.2 1.2 copy-done.1
  2.5 1.2 copy-done.2
  3.7 1.0 shard_map.55
  4.7 3.0 %collective-permute-start.4 = (f32[3,2,4,24,128]{4,3,2,1,0:T(8,128)S(1)}, f32[3,2,4,24,128]{4,3,2,1,0:T(8,128)S(1)}, u32[]{:S(2)}, u32[]{:S(2)}) collective-permute-start(f32[3,2,4,24,128]{4,3,2,1,0:T(8,128)S(1)} %get-tuple-element.15.refs_4_), channel_id=1, source_target_pairs={{0,2},{1,3},{2,0},{3,1},{4,6},{5,7},{6,4},{7,5},{8,10},{9,11},{10,... | collective-permute-start | bytes 884744 | tf_op jit(solution)/shard_map/ppermute | solution.py:215
  7.7 0.0 collective-permute-start.2
  7.7 7.8 %collective-permute-done.4.refs_9_.refs_10_ = f32[3,2,4,24,128]{4,3,2,1,0:T(8,128)S(1)} collective-permute-done((f32[3,2,4,24,128]{4,3,2,1,0:T(8,128)S(1)}, f32[3,2,4,24,128]{4,3,2,1,0:T(8,128)S(1)}, u32[]{:S(2)}, u32[]{:S(2)}) %collective-permute-start.4) | collective-permute-done | bytes 294944 | tf_op jit(solution)/shard_map/ppermute | solution.py:215
  15.5 5.5 %collective-permute-done.2.refs_11_.refs_12_ = f32[3,2,4,24,128]{4,3,2,1,0:T(8,128)S(1)} collective-permute-done((f32[3,2,4,24,128]{4,3,2,1,0:T(8,128)S(1)}, f32[3,2,4,24,128]{4,3,2,1,0:T(8,128)S(1)}, u32[]{:S(2)}, u32[]{:S(2)}) %collective-permute-start.2) | collective-permute-done | bytes 294944 | tf_op jit(solution)/shard_map/ppermute | solution.py:215
  21.0 1.7 %collective-permute-start.5 = (f32[2,2,4,80,128]{4,3,2,1,0:T(8,128)}, f32[2,2,4,80,128]{4,3,2,1,0:T(8,128)}, u32[]{:S(2)}, u32[]{:S(2)}) collective-permute-start(f32[2,2,4,80,128]{4,3,2,1,0:T(8,128)} %get-tuple-element.19.refs_5_), channel_id=1, source_target_pairs={{0,2},{1,3},{2,0},{3,1},{4,6},{5,7},{6,4},{7,5},{8,10},{9,11},{10,... | collective-permute-start | bytes 1966088 | tf_op jit(solution)/shard_map/ppermute | solution.py:215
  22.8 0.0 collective-permute-start.12
  22.8 3.4 %collective-permute-start = (f32[3,2,4,24,128]{4,3,2,1,0:T(8,128)S(1)}, f32[3,2,4,24,128]{4,3,2,1,0:T(8,128)S(1)}, u32[]{:S(2)}, u32[]{:S(2)}) collective-permute-start(f32[3,2,4,24,128]{4,3,2,1,0:T(8,128)S(1)} %get-tuple-element.14.refs_6_), channel_id=1, source_target_pairs={{0,4},{4,8},{8,12},{12,16},{16,20},{20,24},{24,28},{1,5},{5,9},{9,... | collective-permute-start | bytes 884744 | tf_op jit(solution)/shard_map/ppermute | solution.py:218
  26.2 0.3 collective-permute-start.10
  26.5 1.3 collective-permute-start.1
  27.7 0.0 collective-permute-done.12.refs_16_.refs_18_
  27.8 0.3 collective-permute-start.15
  28.1 11.3 %collective-permute-done.refs_3_ = f32[3,2,4,24,128]{4,3,2,1,0:T(8,128)S(1)} collective-permute-done((f32[3,2,4,24,128]{4,3,2,1,0:T(8,128)S(1)}, f32[3,2,4,24,128]{4,3,2,1,0:T(8,128)S(1)}, u32[]{:S(2)}, u32[]{:S(2)}) %collective-permute-start) | collective-permute-done | bytes 294944 | tf_op jit(solution)/shard_map/ppermute | solution.py:218
  39.4 1.3 collective-permute-start.7
  40.7 0.0 collective-permute-done.10.refs_14_.refs_16_
  40.7 0.1 collective-permute-start.17
  40.8 0.0 collective-permute-done.1.refs_7_
  40.8 0.5 collective-permute-start.11
  41.3 0.1 collective-permute-start.16
  41.4 0.0 collective-permute-done.15.refs_19_.refs_22_
  41.4 0.7 copy-done.3
  42.1 0.5 collective-permute-start.6
  42.6 8.2 %collective-permute-done.7.refs_12_.refs_13_ = f32[3,2,4,24,128]{4,3,2,1,0:T(8,128)} collective-permute-done((f32[3,2,4,24,128]{4,3,2,1,0:T(8,128)S(1)}, f32[3,2,4,24,128]{4,3,2,1,0:T(8,128)}, u32[]{:S(2)}, u32[]{:S(2)}) %collective-permute-start.7) | collective-permute-done | bytes 294944 | tf_op jit(solution)/shard_map/ppermute | solution.py:221
  50.8 5.3 %collective-permute-start.3 = (f32[3,2,4,24,128]{4,3,2,1,0:T(8,128)S(1)}, f32[3,2,4,24,128]{4,3,2,1,0:T(8,128)}, u32[]{:S(2)}, u32[]{:S(2)}) collective-permute-start(f32[3,2,4,24,128]{4,3,2,1,0:T(8,128)S(1)} %collective-permute-done.2.refs_11_.refs_12_), channel_id=1, source_target_pairs={{0,4},{4,8},{8,12},{12,16},{16,20},{20,24},{24,28},{1,5},{5,9},{9,... | collective-permute-start | bytes 884744 | tf_op jit(solution)/shard_map/ppermute | solution.py:218
  56.0 0.7 copy-done.6
  56.8 3.8 %collective-permute-done.3.refs_8_.refs_9_ = f32[3,2,4,24,128]{4,3,2,1,0:T(8,128)} collective-permute-done((f32[3,2,4,24,128]{4,3,2,1,0:T(8,128)S(1)}, f32[3,2,4,24,128]{4,3,2,1,0:T(8,128)}, u32[]{:S(2)}, u32[]{:S(2)}) %collective-permute-start.3) | collective-permute-done | bytes 294944 | tf_op jit(solution)/shard_map/ppermute | solution.py:218
  60.6 0.7 copy-done.9
  61.3 0.5 collective-permute-start.18
  61.8 0.0 collective-permute-start.14
  61.8 0.8 copy.7.refs_0_
  62.6 0.1 pad_add_fusion.refs_2_
  62.6 0.5 collective-permute-start.20
  63.2 0.5 collective-permute-start.8
  63.7 0.1 collective-permute-done.14.refs_18_.refs_21_
  63.8 1.0 copy-done.4
  64.7 1.0 copy-done.7
  65.7 1.0 copy-done.10
  66.7 0.7 copy-done.11
  67.3 34.4 %shard_map.56.refs_27_ = f32[8,2,16,16,8,128]{5,4,3,2,1,0:T(8,128)} custom-call(s32[32,2]{1,0:T(8,128)S(1)} %copy.7.refs_0_, s32[4]{0:T(128)S(1)} %copy-done.11, s32[4]{0:T(128)S(1)} %pad_add_fusion.refs_2_, f32[3,2,4,24,128]{4,3,2,1,0:T(8,128)S(1)} %collective-permute-done.refs_3_, f32[3,2,4,24,128]{4,3,2,1,0:T(8,128)S(1)} %get-tuple-element.15.refs_4_, ...), custom_call_target="tpu_custom_call" | custom-call | flops 16000000000 | bytes 33554432 | tf_op jit(solution)/shard_map/pallas_call | solution.py:187
  101.7 0.6 collective-permute-start.22
  102.4 0.1 collective-permute-start.19
  102.4 0.4 collective-permute-start.21
  102.9 1.5 %collective-permute-done.19.refs_17_ = f32[1,2,4,80,128]{4,3,2,1,0:T(8,128)S(1)} collective-permute-done((f32[1,2,4,80,128]{4,3,2,1,0:T(8,128)S(1)}, f32[1,2,4,80,128]{4,3,2,1,0:T(8,128)S(1)}, u32[]{:S(2)}, u32[]{:S(2)}) %collective-permute-start.19) | collective-permute-done | bytes 327712 | tf_op jit(solution)/shard_map/ppermute | solution.py:215
  104.4 0.5 collective-permute-done.21.refs_23_
  104.8 24.7 %shard_map.57 = f32[8,16,16,8,128]{4,3,2,1,0:T(8,128)} custom-call(s32[32,2]{1,0:T(8,128)S(1)} %copy.7.refs_0_, s32[4]{0:T(128)S(1)} %copy-done.12, s32[4]{0:T(128)S(1)} %pad_add_fusion.refs_2_, f32[3,2,4,24,128]{4,3,2,1,0:T(8,128)S(1)} %collective-permute-done.refs_3_, f32[3,2,4,24,128]{4,3,2,1,0:T(8,128)S(1)} %get-tuple-element.15.refs_4_, ...), custom_call_target="tpu_custom_call" | custom-call | flops 8000000000 | bytes 16777216 | tf_op jit(solution)/shard_map/pallas_call | solution.py:187
  (29 shorter events, 0.1 us)
Async XLA Ops:
  0.0 1.2 copy-start
  1.2 1.2 copy-start.1
  2.5 1.2 copy-start.2
  4.7 10.8 %collective-permute-start.4 = (f32[3,2,4,24,128]{4,3,2,1,0:T(8,128)S(1)}, f32[3,2,4,24,128]{4,3,2,1,0:T(8,128)S(1)}, u32[]{:S(2)}, u32[]{:S(2)}) collective-permute-start(f32[3,2,4,24,128]{4,3,2,1,0:T(8,128)S(1)} %get-tuple-element.15.refs_4_), channel_id=1, source_target_pairs={{0,2},{1,3},{2,0},{3,1},{4,6},{5,7},{6,4},{7,5},{8,10},{9,11},{10,... | collective-permute-start | bytes 884744 | tf_op jit(solution)/shard_map/ppermute | solution.py:215
  7.7 13.3 %collective-permute-start.2 = (f32[3,2,4,24,128]{4,3,2,1,0:T(8,128)S(1)}, f32[3,2,4,24,128]{4,3,2,1,0:T(8,128)S(1)}, u32[]{:S(2)}, u32[]{:S(2)}) collective-permute-start(f32[3,2,4,24,128]{4,3,2,1,0:T(8,128)S(1)} %get-tuple-element.14.refs_6_), channel_id=1, source_target_pairs={{0,2},{1,3},{2,0},{3,1},{4,6},{5,7},{6,4},{7,5},{8,10},{9,11},{10,... | collective-permute-start | bytes 884744 | tf_op jit(solution)/shard_map/ppermute | solution.py:215
  21.0 20.3 %collective-permute-start.5 = (f32[2,2,4,80,128]{4,3,2,1,0:T(8,128)}, f32[2,2,4,80,128]{4,3,2,1,0:T(8,128)}, u32[]{:S(2)}, u32[]{:S(2)}) collective-permute-start(f32[2,2,4,80,128]{4,3,2,1,0:T(8,128)} %get-tuple-element.19.refs_5_), channel_id=1, source_target_pairs={{0,2},{1,3},{2,0},{3,1},{4,6},{5,7},{6,4},{7,5},{8,10},{9,11},{10,... | collective-permute-start | bytes 1966088 | tf_op jit(solution)/shard_map/ppermute | solution.py:215
  22.8 5.0 %collective-permute-start.12 = (f32[3,2,4,24,128]{4,3,2,1,0:T(8,128)S(1)}, f32[3,2,4,24,128]{4,3,2,1,0:T(8,128)S(1)}, u32[]{:S(2)}, u32[]{:S(2)}) collective-permute-start(f32[3,2,4,24,128]{4,3,2,1,0:T(8,128)S(1)} %get-tuple-element.14.refs_6_), channel_id=1, source_target_pairs={{0,1},{1,0},{2,3},{3,2},{4,5},{5,4},{6,7},{7,6},{8,9},{9,8},{10,11... | collective-permute-start | bytes 884744 | tf_op jit(solution)/shard_map/ppermute | solution.py:215
  22.8 16.6 %collective-permute-start = (f32[3,2,4,24,128]{4,3,2,1,0:T(8,128)S(1)}, f32[3,2,4,24,128]{4,3,2,1,0:T(8,128)S(1)}, u32[]{:S(2)}, u32[]{:S(2)}) collective-permute-start(f32[3,2,4,24,128]{4,3,2,1,0:T(8,128)S(1)} %get-tuple-element.14.refs_6_), channel_id=1, source_target_pairs={{0,4},{4,8},{8,12},{12,16},{16,20},{20,24},{24,28},{1,5},{5,9},{9,... | collective-permute-start | bytes 884744 | tf_op jit(solution)/shard_map/ppermute | solution.py:218
  26.2 14.5 %collective-permute-start.10 = (f32[3,2,4,24,128]{4,3,2,1,0:T(8,128)S(1)}, f32[3,2,4,24,128]{4,3,2,1,0:T(8,128)S(1)}, u32[]{:S(2)}, u32[]{:S(2)}) collective-permute-start(f32[3,2,4,24,128]{4,3,2,1,0:T(8,128)S(1)} %get-tuple-element.15.refs_4_), channel_id=1, source_target_pairs={{0,1},{1,0},{2,3},{3,2},{4,5},{5,4},{6,7},{7,6},{8,9},{9,8},{10,11... | collective-permute-start | bytes 884744 | tf_op jit(solution)/shard_map/ppermute | solution.py:215
  26.5 14.3 %collective-permute-start.1 = (f32[3,2,4,24,128]{4,3,2,1,0:T(8,128)S(1)}, f32[3,2,4,24,128]{4,3,2,1,0:T(8,128)S(1)}, u32[]{:S(2)}, u32[]{:S(2)}) collective-permute-start(f32[3,2,4,24,128]{4,3,2,1,0:T(8,128)S(1)} %get-tuple-element.15.refs_4_), channel_id=1, source_target_pairs={{4,0},{8,4},{12,8},{16,12},{20,16},{24,20},{28,24},{5,1},{9,5},{13... | collective-permute-start | bytes 884744 | tf_op jit(solution)/shard_map/ppermute | solution.py:221
  27.8 13.6 %collective-permute-start.15 = (f32[3,2,4,24,128]{4,3,2,1,0:T(8,128)S(1)}, f32[3,2,4,24,128]{4,3,2,1,0:T(8,128)S(1)}, u32[]{:S(2)}, u32[]{:S(2)}) collective-permute-start(f32[3,2,4,24,128]{4,3,2,1,0:T(8,128)S(1)} %collective-permute-done.4.refs_9_.refs_10_), channel_id=1, source_target_pairs={{0,1},{1,0},{2,3},{3,2},{4,5},{5,4},{6,7},{7,6},{8,9},{9,8},{10,11... | collective-permute-start | bytes 884744 | tf_op jit(solution)/shard_map/ppermute | solution.py:215
  39.4 11.4 %collective-permute-start.7 = (f32[3,2,4,24,128]{4,3,2,1,0:T(8,128)S(1)}, f32[3,2,4,24,128]{4,3,2,1,0:T(8,128)}, u32[]{:S(2)}, u32[]{:S(2)}) collective-permute-start(f32[3,2,4,24,128]{4,3,2,1,0:T(8,128)S(1)} %collective-permute-done.4.refs_9_.refs_10_), channel_id=1, source_target_pairs={{4,0},{8,4},{12,8},{16,12},{20,16},{24,20},{28,24},{5,1},{9,5},{13... | collective-permute-start | bytes 884744 | tf_op jit(solution)/shard_map/ppermute | solution.py:221
  40.7 15.4 %collective-permute-start.17 = (f32[3,2,4,24,128]{4,3,2,1,0:T(8,128)S(1)}, f32[3,2,4,24,128]{4,3,2,1,0:T(8,128)S(1)}, u32[]{:S(2)}, u32[]{:S(2)}) collective-permute-start(f32[3,2,4,24,128]{4,3,2,1,0:T(8,128)S(1)} %collective-permute-done.2.refs_11_.refs_12_), channel_id=1, source_target_pairs={{0,1},{1,0},{2,3},{3,2},{4,5},{5,4},{6,7},{7,6},{8,9},{9,8},{10,11... | collective-permute-start | bytes 884744 | tf_op jit(solution)/shard_map/ppermute | solution.py:215
  40.8 22.4 %collective-permute-start.11 = (f32[2,2,4,80,128]{4,3,2,1,0:T(8,128)}, f32[2,2,4,80,128]{4,3,2,1,0:T(8,128)}, u32[]{:S(2)}, u32[]{:S(2)}) collective-permute-start(f32[2,2,4,80,128]{4,3,2,1,0:T(8,128)} %get-tuple-element.19.refs_5_), channel_id=1, source_target_pairs={{0,1},{1,0},{2,3},{3,2},{4,5},{5,4},{6,7},{7,6},{8,9},{9,8},{10,11... | collective-permute-start | bytes 1966088 | tf_op jit(solution)/shard_map/ppermute | solution.py:215
  41.3 22.5 %collective-permute-start.16 = (f32[2,2,4,80,128]{4,3,2,1,0:T(8,128)}, f32[2,2,4,80,128]{4,3,2,1,0:T(8,128)}, u32[]{:S(2)}, u32[]{:S(2)}) collective-permute-start(f32[2,2,4,80,128]{4,3,2,1,0:T(8,128)} %collective-permute-done.5.refs_10_), channel_id=1, source_target_pairs={{0,1},{1,0},{2,3},{3,2},{4,5},{5,4},{6,7},{7,6},{8,9},{9,8},{10,11... | collective-permute-start | bytes 1966088 | tf_op jit(solution)/shard_map/ppermute | solution.py:215
  41.4 0.7 copy-start.3
  42.1 19.7 %collective-permute-start.6 = (f32[1,2,4,80,128]{4,3,2,1,0:T(8,128)S(1)}, f32[1,2,4,80,128]{4,3,2,1,0:T(8,128)S(1)}, u32[]{:S(2)}, u32[]{:S(2)}) collective-permute-start(f32[1,2,4,80,128]{4,3,2,1,0:T(8,128)S(1)} %get-tuple-element.20.refs_5_), channel_id=1, source_target_pairs={{0,2},{1,3},{2,0},{3,1},{4,6},{5,7},{6,4},{7,5},{8,10},{9,11},{10,... | collective-permute-start | bytes 983048 | tf_op jit(solution)/shard_map/ppermute | solution.py:215
  50.8 9.8 %collective-permute-start.3 = (f32[3,2,4,24,128]{4,3,2,1,0:T(8,128)S(1)}, f32[3,2,4,24,128]{4,3,2,1,0:T(8,128)}, u32[]{:S(2)}, u32[]{:S(2)}) collective-permute-start(f32[3,2,4,24,128]{4,3,2,1,0:T(8,128)S(1)} %collective-permute-done.2.refs_11_.refs_12_), channel_id=1, source_target_pairs={{0,4},{4,8},{8,12},{12,16},{16,20},{20,24},{24,28},{1,5},{5,9},{9,... | collective-permute-start | bytes 884744 | tf_op jit(solution)/shard_map/ppermute | solution.py:218
  56.0 0.7 copy-start.6
  56.8 3.8 %collective-permute-start.9 = (f32[3,2,4,24,128]{4,3,2,1,0:T(8,128)S(1)}, f32[3,2,4,24,128]{4,3,2,1,0:T(8,128)S(1)}, u32[]{:S(2)}, u32[]{:S(2)}) collective-permute-start(f32[3,2,4,24,128]{4,3,2,1,0:T(8,128)S(1)} %collective-permute-done.refs_3_), channel_id=1, source_target_pairs={{0,1},{1,0},{2,3},{3,2},{4,5},{5,4},{6,7},{7,6},{8,9},{9,8},{10,11... | collective-permute-start | bytes 884744 | tf_op jit(solution)/shard_map/ppermute | solution.py:215
  60.6 2.1 %collective-permute-start.13 = (f32[3,2,4,24,128]{4,3,2,1,0:T(8,128)S(1)}, f32[3,2,4,24,128]{4,3,2,1,0:T(8,128)}, u32[]{:S(2)}, u32[]{:S(2)}) collective-permute-start(f32[3,2,4,24,128]{4,3,2,1,0:T(8,128)S(1)} %collective-permute-done.1.refs_7_), channel_id=1, source_target_pairs={{0,1},{1,0},{2,3},{3,2},{4,5},{5,4},{6,7},{7,6},{8,9},{9,8},{10,11... | collective-permute-start | bytes 884744 | tf_op jit(solution)/shard_map/ppermute | solution.py:215
  60.6 0.7 copy-start.9
  61.3 2.4 %collective-permute-start.18 = (f32[3,2,4,24,128]{4,3,2,1,0:T(8,128)}, f32[3,2,4,24,128]{4,3,2,1,0:T(8,128)}, u32[]{:S(2)}, u32[]{:S(2)}) collective-permute-start(f32[3,2,4,24,128]{4,3,2,1,0:T(8,128)} %collective-permute-done.7.refs_12_.refs_13_), channel_id=1, source_target_pairs={{0,1},{1,0},{2,3},{3,2},{4,5},{5,4},{6,7},{7,6},{8,9},{9,8},{10,11... | collective-permute-start | bytes 884744 | tf_op jit(solution)/shard_map/ppermute | solution.py:215
  61.8 2.0 %collective-permute-start.14 = (f32[3,2,4,24,128]{4,3,2,1,0:T(8,128)}, f32[3,2,4,24,128]{4,3,2,1,0:T(8,128)}, u32[]{:S(2)}, u32[]{:S(2)}) collective-permute-start(f32[3,2,4,24,128]{4,3,2,1,0:T(8,128)} %collective-permute-done.3.refs_8_.refs_9_), channel_id=1, source_target_pairs={{0,1},{1,0},{2,3},{3,2},{4,5},{5,4},{6,7},{7,6},{8,9},{9,8},{10,11... | collective-permute-start | bytes 884744 | tf_op jit(solution)/shard_map/ppermute | solution.py:215
  62.6 42.2 %copy-start.12 = (s32[4]{0:T(128)S(1)}, s32[4]{0:T(128)}, u32[]{:S(2)}) copy-start(s32[4]{0:T(128)} %refs_1_.3) | copy-start | bytes 52
  62.6 41.7 %collective-permute-start.20 = (f32[2,4,128,128]{3,2,1,0:T(8,128)S(1)}, f32[2,4,128,128]{3,2,1,0:T(8,128)S(1)}, u32[]{:S(2)}, u32[]{:S(2)}) collective-permute-start(f32[2,4,128,128]{3,2,1,0:T(8,128)S(1)} %get-tuple-element.21.refs_8_), channel_id=1, source_target_pairs={{0,1},{1,0},{2,3},{3,2},{4,5},{5,4},{6,7},{7,6},{8,9},{9,8},{10,11... | collective-permute-start | bytes 1572872 | tf_op jit(solution)/shard_map/ppermute | solution.py:215
  63.2 38.5 %collective-permute-start.8 = (f32[2,4,128,128]{3,2,1,0:T(8,128)S(1)}, f32[2,4,128,128]{3,2,1,0:T(8,128)S(1)}, u32[]{:S(2)}, u32[]{:S(2)}) collective-permute-start(f32[2,4,128,128]{3,2,1,0:T(8,128)S(1)} %get-tuple-element.21.refs_8_), channel_id=1, source_target_pairs={{0,2},{1,3},{2,0},{3,1},{4,6},{5,7},{6,4},{7,5},{8,10},{9,11},{10,... | collective-permute-start | bytes 1572872 | tf_op jit(solution)/shard_map/ppermute | solution.py:215
  63.8 1.0 copy-start.4
  64.7 1.0 copy-start.7
  65.7 1.0 copy-start.10
  66.7 0.7 copy-start.11
  67.3 37.5 %copy-start.5 = (f32[3,2,4,24,128]{4,3,2,1,0:T(8,128)S(1)}, f32[3,2,4,24,128]{4,3,2,1,0:T(8,128)}, u32[]{:S(2)}) copy-start(f32[3,2,4,24,128]{4,3,2,1,0:T(8,128)} %copy-done.3) | copy-start | bytes 884740
  67.3 37.5 %copy-start.8 = (f32[3,2,4,24,128]{4,3,2,1,0:T(8,128)S(1)}, f32[3,2,4,24,128]{4,3,2,1,0:T(8,128)}, u32[]{:S(2)}) copy-start(f32[3,2,4,24,128]{4,3,2,1,0:T(8,128)} %copy-done.6) | copy-start | bytes 884740
  101.7 3.1 %collective-permute-start.22 = (f32[2,4,128,128]{3,2,1,0:T(8,128)S(1)}, f32[2,4,128,128]{3,2,1,0:T(8,128)S(1)}, u32[]{:S(2)}, u32[]{:S(2)}) collective-permute-start(f32[2,4,128,128]{3,2,1,0:T(8,128)S(1)} %collective-permute-done.8.refs_14_), channel_id=1, source_target_pairs={{0,1},{1,0},{2,3},{3,2},{4,5},{5,4},{6,7},{7,6},{8,9},{9,8},{10,11... | collective-permute-start | bytes 1572872 | tf_op jit(solution)/shard_map/ppermute | solution.py:215
  102.4 2.0 %collective-permute-start.19 = (f32[1,2,4,80,128]{4,3,2,1,0:T(8,128)S(1)}, f32[1,2,4,80,128]{4,3,2,1,0:T(8,128)S(1)}, u32[]{:S(2)}, u32[]{:S(2)}) collective-permute-start(f32[1,2,4,80,128]{4,3,2,1,0:T(8,128)S(1)} %get-tuple-element.20.refs_5_), channel_id=1, source_target_pairs={{0,1},{1,0},{2,3},{3,2},{4,5},{5,4},{6,7},{7,6},{8,9},{9,8},{10,11... | collective-permute-start | bytes 983048 | tf_op jit(solution)/shard_map/ppermute | solution.py:215
  102.4 2.4 %collective-permute-start.21 = (f32[1,2,4,80,128]{4,3,2,1,0:T(8,128)S(1)}, f32[1,2,4,80,128]{4,3,2,1,0:T(8,128)S(1)}, u32[]{:S(2)}, u32[]{:S(2)}) collective-permute-start(f32[1,2,4,80,128]{4,3,2,1,0:T(8,128)S(1)} %collective-permute-done.6.refs_11_), channel_id=1, source_target_pairs={{0,1},{1,0},{2,3},{3,2},{4,5},{5,4},{6,7},{7,6},{8,9},{9,8},{10,11... | collective-permute-start | bytes 983048 | tf_op jit(solution)/shard_map/ppermute | solution.py:215

commit v3 on v1

--- a/solution.py
+++ b/solution.py
@@ -54,24 +54,31 @@
 
     @pl.when(step == 0)
     def _():
-        copies = []
+        waves = [[] for _ in range(later + 1)]
+        started = 0
+        for exposure in range(later):
+            for piece in range(pieces):
+                above, edges, mid, below, _ = piece_refs[5 * piece : 5 * piece + 5]
+                place = owner_ref[piece] * tiles
+                moves = (
+                    (above.at[exposure], 0, REACH),
+                    (edges.at[0, exposure], REACH, REACH),
+                    (mid.at[exposure], 2 * REACH, rows - 2 * REACH),
+                    (edges.at[1, exposure], rows, REACH),
+                    (below.at[exposure], rows + REACH, REACH),
+                )
+                for source, start, count in moves:
+                    target = image.at[exposure, :, 0, pl.ds(1 + place, tiles), pl.ds(start, count), :]
+                    waves[exposure].append(pltpu.make_async_copy(source, target, sems.at[started]))
+                    started += 1
         for piece in range(pieces):
-            above, edges, mid, below, own_first = piece_refs[5 * piece : 5 * piece + 5]
-            place = owner_ref[piece] * tiles
-            moves = (
-                (above, 0, REACH),
-                (edges.at[0], REACH, REACH),
-                (mid, 2 * REACH, rows - 2 * REACH),
-                (edges.at[1], rows, REACH),
-                (below, rows + REACH, REACH),
-            )
-            for source, start, count in moves:
-                target = image.at[:, :, 0, pl.ds(1 + place, tiles), pl.ds(start, count), :]
-                copies.append(pltpu.make_async_copy(source, target, sems.at[len(copies)]))
-            target = first.at[:, pl.ds(place, tiles)]
-            copies.append(pltpu.make_async_copy(own_first, target, sems.at[len(copies)]))
-        for copy in copies:
-            copy.start()
+            target = first.at[:, pl.ds(owner_ref[piece] * tiles, tiles)]
+            source = piece_refs[5 * piece + 4]
+            waves[later].append(pltpu.make_async_copy(source, target, sems.at[started]))
+            started += 1
+        for wave in waves:
+            for copy in wave:
+                copy.start()
         depth = image.shape[4]
         blank = jnp.zeros((depth, LANES), jnp.float32)
         for exposure in range(later):
@@ -81,27 +88,25 @@
                     image[exposure, layer, part, all_tiles + 1] = blank
                 for tile in range(all_tiles):
                     image[exposure, layer, 0, tile + 1, rows + 2 * REACH :] = blank[rows + 2 * REACH :]
-        for copy in copies:
+        groups = depth // 8
+
+        def interpolate(exposure, index, carry):
+            layer = index // groups
+            here = pl.ds(pl.multiple_of(index % groups * 8, 8), 8)
+            values = [image[exposure, layer, 0, tile, here, :] for tile in range(all_tiles + 2)]
+            moved = [pltpu.roll(value, LANES - 1, 1) for value in values]
+            for tile in range(all_tiles + 1):
+                slope = jnp.where(lane < LANES - 1, moved[tile], moved[tile + 1]) - values[tile]
+                for part in range(1, 4):
+                    image[exposure, layer, part, tile, here, :] = values[tile] + (0.25 * part) * slope
+            return carry
+
+        for exposure in range(later):
+            for copy in waves[exposure]:
+                copy.wait()
+            lax.fori_loop(0, 2 * groups, functools.partial(interpolate, exposure), 0)
+        for copy in waves[later]:
             copy.wait()
-        wide_lane = lax.broadcasted_iota(jnp.int32, (depth, LANES), 1)
-
-        def interpolate(index, carry):
-            exposure = index // (2 * (all_tiles + 1))
-            layer = index // (all_tiles + 1) % 2
-            tile = index % (all_tiles + 1)
-            left = image[exposure, layer, 0, tile]
-            right = image[exposure, layer, 0, tile + 1]
-            moved = jnp.where(
-                wide_lane < LANES - 1,
-                pltpu.roll(left, LANES - 1, 1),
-                pltpu.roll(right, LANES - 1, 1),
-            )
-            slope = moved - left
-            for part in range(1, 4):
-                image[exposure, layer, part, tile] = left + (0.25 * part) * slope
-            return carry
-
-        lax.fori_loop(0, later * 2 * (all_tiles + 1), interpolate, 0)
 
     index = owner_ref[0] * per_device + step
     plans = []
@@ -131,13 +136,16 @@
 
         lanes = [(e, l) for e in range(later) for l in range(2)]
         held = {key: turned(*key, 0) for key in lanes}
+        done = []
         for tile in range(all_tiles):
             total = [first[layer, tile, pl.ds(pl.multiple_of(8 * group, 8), 8), :] for layer in range(2)]
             for key in lanes:
                 following = turned(*key, tile + 1)
                 total[key[1]] += jnp.where(plans[key[0]][5], held[key], following)
                 held[key] = following
-            out_ref[0, group, tile] = total[0] * lax.rsqrt(jnp.maximum(total[1], 1.0))
+            done.append(total[0] * lax.rsqrt(jnp.maximum(total[1], 1.0)))
+        for tile in range(all_tiles):
+            out_ref[0, group, tile] = done[tile]
         return carry
 
     lax.fori_loop(0, rows // 8, row_group, 0)
@@ -161,7 +169,7 @@
         scratch_shapes=[
             pltpu.VMEM((later, 2, 4, all_tiles + 2, depth, LANES), jnp.float32),
             pltpu.VMEM((2, all_tiles, rows, LANES), jnp.float32),
-            pltpu.SemaphoreType.DMA((6 * count,)),
+            pltpu.SemaphoreType.DMA(((5 * later + 1) * count,)),
         ],
         compiler_params=pltpu.CompilerParams(vmem_limit_bytes=56 * MIB),
     )(velocities, time_offsets, owners, *flat)
@@ -189,14 +197,19 @@
         return lax.ppermute(value, "sky", [(i + 1, i) for i in range(skies - 1)])
 
     far = [2 * k for k in range(1, count // 2)]
+    above, below = from_rows_above(edges[1]), from_rows_below(edges[0])
     far_edges = [edges] + [swap(edges, bits) for bits in far]
-    far_mid = [mid] + [swap(after(mid, far_edges[-1]), bits) for bits in far]
-    far_first = [first] + [swap(after(first, far_mid[-1]), bits) for bits in far]
+    sent = after(mid, far_edges[-1], above, below)
+    far_mid = [mid] + [swap(sent, bits) for bits in far]
+    above, below = [above], [below]
+    for value in far_edges[1:]:
+        above.append(from_rows_above(value[1]))
+        below.append(from_rows_below(value[0]))
+    sent = after(first, far_mid[-1], above[-1], below[-1])
+    far_first = [first] + [swap(sent, bits) for bits in far]
     pieces, owners = [], []
     for k in range(count // 2):
-        above = from_rows_above(far_edges[k][1])
-        below = from_rows_below(far_edges[k][0])
-        pieces.append((above, far_edges[k], far_mid[k], below, far_first[k]))
+        pieces.append((above[k], far_edges[k], far_mid[k], below[k], far_first[k]))
         owners.append(me ^ (2 * k))
     for k in range(count // 2):
         pieces.append(tuple(swap(array, 1) for array in pieces[k]))

time: 113 us -> 108 us (0.956)
  Pallas kernels: 45.1 us -> 43.3 us
  local copies, waits for them, and re-layouts: 7.64 us -> 6.11 us
  starting transfers between devices: 20 us -> 18.6 us
    ppermute x13, waiting for transfers between devices: 19.6 us -> 17.3 us  [swap(): return lax.ppermute(value, 'vel', [(i, i ^ bits) for i in range(count)])]
    ppermute x13, starting transfers between devices: 7.57 us -> 5.7 us  [swap(): return lax.ppermute(value, 'vel', [(i, i ^ bits) for i in range(count)])]
    pallas_call x1, Pallas kernels: 44.9 us -> 43.1 us  [stack(): pl.pallas_call(functools.partial(stack_kernel, count, tiles, later, rows,...]
    ppermute x2, waiting for transfers between devices: 11.1 us -> 12.6 us  [from_rows_above(): return lax.ppermute(value, 'sky', [(i, i + 1) for i in range(skies - 1)])]
    unnamed x29, local copies, waits for them, and re-layouts: 7.56 us -> 6.03 us
where the time goes in v3:
time: 108 us; the launch traced here: 107 us
  Pallas kernels  43.3 us (40%)
  waiting for transfers between devices  38.5 us (36%)
  starting transfers between devices  18.6 us (17%)
  local copies, waits for them, and re-layouts  6.11 us (6%)
    pallas_call x1, Pallas kernels, stack(): pl.pallas_call(functools.partial(stack_kernel, count, tiles, later, rows,...  43.1 us
    ppermute x13, waiting for transfers between devices, swap(): return lax.ppermute(value, 'vel', [(i, i ^ bits) for i in range(count)])  17.3 us
    ppermute x2, waiting for transfers between devices, from_rows_above(): return lax.ppermute(value, 'sky', [(i, i + 1) for i in range(skies - 1)])  12.6 us
    ppermute x2, starting transfers between devices, from_rows_above(): return lax.ppermute(value, 'sky', [(i, i + 1) for i in range(skies - 1)])  10.3 us
    ppermute x2, waiting for transfers between devices, from_rows_below(): return lax.ppermute(value, 'sky', [(i + 1, i) for i in range(skies - 1)])  8.58 us
    unnamed x29, local copies, waits for them, and re-layouts  6.03 us
    ppermute x13, starting transfers between devices, swap(): return lax.ppermute(value, 'vel', [(i, i ^ bits) for i in range(count)])  5.7 us
    ppermute x2, starting transfers between devices, from_rows_below(): return lax.ppermute(value, 'sky', [(i + 1, i) for i in range(skies - 1)])  2.58 us
  transfers between devices with their start and end apart: 17, of which 7 were waited for; matrix products, arithmetic and copies ran while one was open for 2% of the time, Pallas kernels for 0%

profile of v3, /device:TPU:0, one launch (start us, length us, event | category | flops | bytes accessed | tf_op | source)
XLA Modules:
  0.0 107.3 jit_solution(3865490128365549870)
XLA Ops:
  0.0 1.2 %copy-done.1 = f32[4,128,512]{2,1,0:T(8,128)S(1)} copy-done((f32[4,128,512]{2,1,0:T(8,128)S(1)}, f32[4,128,512]{2,1,0:T(8,128)}, u32[]{:S(2)}) %copy-start.1) | copy-done | bytes 1048600
  1.2 1.2 %copy-done.2 = f32[4,128,512]{2,1,0:T(8,128)S(1)} copy-done((f32[4,128,512]{2,1,0:T(8,128)S(1)}, f32[4,128,512]{2,1,0:T(8,128)}, u32[]{:S(2)}) %copy-start.2) | copy-done | bytes 1048600
  2.5 1.2 %copy-done.3 = s32[4,128,512]{2,1,0:T(8,128)S(1)} copy-done((s32[4,128,512]{2,1,0:T(8,128)S(1)}, s32[4,128,512]{2,1,0:T(8,128)}, u32[]{:S(2)}) %copy-start.3) | copy-done | bytes 1048600
  3.7 0.2 shard_map.55
  3.9 0.0 copy-start
  3.9 0.0 copy-start.4
  3.9 0.0 copy-start.5
  3.9 3.0 %collective-permute-start.2 = (f32[2,3,2,4,24,128]{5,4,3,2,1,0:T(8,128)S(1)}, f32[2,3,2,4,24,128]{5,4,3,2,1,0:T(8,128)S(1)}, u32[]{:S(2)}, u32[]{:S(2)}) collective-permute-start(f32[2,3,2,4,24,128]{5,4,3,2,1,0:T(8,128)S(1)} %get-tuple-element.10.refs_4_), channel_id=1, source_target_pairs={{0,2},{1,3},{2,0},{3,1},{4,6},{5,7},{6,4},{7,5},{8,10},{9,11},{10,... | collective-permute-start | bytes 1769480 | tf_op jit(solution)/shard_map/ppermute | solution.py:191
  7.0 1.3 %collective-permute-start.1 = (f32[3,2,4,24,128]{4,3,2,1,0:T(8,128)S(1)}, f32[3,2,4,24,128]{4,3,2,1,0:T(8,128)S(1)}, u32[]{:S(2)}, u32[]{:S(2)}) collective-permute-start(f32[3,2,4,24,128]{4,3,2,1,0:T(8,128)S(1)} %get-tuple-element.17), channel_id=1, source_target_pairs={{4,0},{8,4},{12,8},{16,12},{20,16},{24,20},{28,24},{5,1},{9,5},{13... | collective-permute-start | bytes 884744 | tf_op jit(solution)/shard_map/ppermute | solution.py:197
  8.3 4.6 %collective-permute-start = (f32[3,2,4,24,128]{4,3,2,1,0:T(8,128)S(1)}, f32[3,2,4,24,128]{4,3,2,1,0:T(8,128)S(1)}, u32[]{:S(2)}, u32[]{:S(2)}) collective-permute-start(f32[3,2,4,24,128]{4,3,2,1,0:T(8,128)S(1)} %get-tuple-element.18), channel_id=1, source_target_pairs={{0,4},{4,8},{8,12},{12,16},{16,20},{20,24},{24,28},{1,5},{5,9},{9,... | collective-permute-start | bytes 884744 | tf_op jit(solution)/shard_map/ppermute | solution.py:194
  12.9 4.5 %collective-permute-done.1.refs_6_ = f32[3,2,4,24,128]{4,3,2,1,0:T(8,128)S(1)} collective-permute-done((f32[3,2,4,24,128]{4,3,2,1,0:T(8,128)S(1)}, f32[3,2,4,24,128]{4,3,2,1,0:T(8,128)S(1)}, u32[]{:S(2)}, u32[]{:S(2)}) %collective-permute-start.1) | collective-permute-done | bytes 294944 | tf_op jit(solution)/shard_map/ppermute | solution.py:197
  17.4 6.2 %collective-permute-done.refs_3_ = f32[3,2,4,24,128]{4,3,2,1,0:T(8,128)S(1)} collective-permute-done((f32[3,2,4,24,128]{4,3,2,1,0:T(8,128)S(1)}, f32[3,2,4,24,128]{4,3,2,1,0:T(8,128)S(1)}, u32[]{:S(2)}, u32[]{:S(2)}) %collective-permute-start) | collective-permute-done | bytes 294944 | tf_op jit(solution)/shard_map/ppermute | solution.py:194
  23.6 0.0 collective-permute-done.2.refs_9_
  23.6 0.5 collective-permute-start.4
  24.2 1.3 %collective-permute-start.5 = (f32[3,2,4,24,128]{4,3,2,1,0:T(8,128)S(1)}, f32[3,2,4,24,128]{4,3,2,1,0:T(8,128)}, u32[]{:S(2)}, u32[]{:S(2)}) collective-permute-start(f32[3,2,4,24,128]{4,3,2,1,0:T(8,128)S(1)} %get-tuple-element.15), channel_id=1, source_target_pairs={{4,0},{8,4},{12,8},{16,12},{20,16},{24,20},{28,24},{5,1},{9,5},{13... | collective-permute-start | bytes 884744 | tf_op jit(solution)/shard_map/ppermute | solution.py:197
  25.5 0.1 collective-permute-start.11
  25.5 5.8 %collective-permute-start.3 = (f32[3,2,4,24,128]{4,3,2,1,0:T(8,128)S(1)}, f32[3,2,4,24,128]{4,3,2,1,0:T(8,128)}, u32[]{:S(2)}, u32[]{:S(2)}) collective-permute-start(f32[3,2,4,24,128]{4,3,2,1,0:T(8,128)S(1)} %get-tuple-element.16), channel_id=1, source_target_pairs={{0,4},{4,8},{8,12},{12,16},{16,20},{20,24},{24,28},{1,5},{5,9},{9,... | collective-permute-start | bytes 884744 | tf_op jit(solution)/shard_map/ppermute | solution.py:194
  31.3 0.2 collective-permute-start.9
  31.5 4.1 %collective-permute-done.5.refs_11_ = f32[3,2,4,24,128]{4,3,2,1,0:T(8,128)} collective-permute-done((f32[3,2,4,24,128]{4,3,2,1,0:T(8,128)S(1)}, f32[3,2,4,24,128]{4,3,2,1,0:T(8,128)}, u32[]{:S(2)}, u32[]{:S(2)}) %collective-permute-start.5) | collective-permute-done | bytes 294944 | tf_op jit(solution)/shard_map/ppermute | solution.py:197
  35.6 0.0 collective-permute-start.10
  35.6 6.4 %collective-permute-done.3.refs_8_ = f32[3,2,4,24,128]{4,3,2,1,0:T(8,128)} collective-permute-done((f32[3,2,4,24,128]{4,3,2,1,0:T(8,128)S(1)}, f32[3,2,4,24,128]{4,3,2,1,0:T(8,128)}, u32[]{:S(2)}, u32[]{:S(2)}) %collective-permute-start.3) | collective-permute-done | bytes 294944 | tf_op jit(solution)/shard_map/ppermute | solution.py:194
  42.0 5.4 %collective-permute-done.4.refs_10_ = f32[3,2,4,80,128]{4,3,2,1,0:T(8,128)} collective-permute-done((f32[3,2,4,80,128]{4,3,2,1,0:T(8,128)S(1)}, f32[3,2,4,80,128]{4,3,2,1,0:T(8,128)}, u32[]{:S(2)}, u32[]{:S(2)}) %collective-permute-start.4) | collective-permute-done | bytes 983072 | tf_op jit(solution)/shard_map/ppermute | solution.py:191
  47.4 0.5 collective-permute-start.6
  47.9 0.0 collective-permute-start.14
  47.9 0.0 collective-permute-done.11.refs_17_
  47.9 0.5 collective-permute-start.8
  48.4 0.0 collective-permute-done.10.refs_16_
  48.4 0.1 collective-permute-start.7
  48.5 3.2 %collective-permute-done.7.refs_13_ = f32[3,2,4,24,128]{4,3,2,1,0:T(8,128)S(1)} collective-permute-done((f32[3,2,4,24,128]{4,3,2,1,0:T(8,128)S(1)}, f32[3,2,4,24,128]{4,3,2,1,0:T(8,128)S(1)}, u32[]{:S(2)}, u32[]{:S(2)}) %collective-permute-start.7) | collective-permute-done | bytes 294944 | tf_op jit(solution)/shard_map/ppermute | solution.py:191
  51.7 0.1 collective-permute-start.13
  51.9 8.6 %collective-permute-done.6.refs_12_ = f32[2,4,128,128]{3,2,1,0:T(8,128)} collective-permute-done((f32[2,4,128,128]{3,2,1,0:T(8,128)S(1)}, f32[2,4,128,128]{3,2,1,0:T(8,128)}, u32[]{:S(2)}, u32[]{:S(2)}) %collective-permute-start.6) | collective-permute-done | bytes 524320 | tf_op jit(solution)/shard_map/ppermute | solution.py:191
  60.5 0.0 collective-permute-start.16
  60.5 0.0 collective-permute-done.8.refs_14_
  60.5 0.5 collective-permute-start.15
  61.0 0.0 collective-permute-done.9.refs_15_
  61.0 1.0 copy-done.7
  62.0 0.1 collective-permute-start.12
  62.1 0.0 copy-done.10
  62.1 0.0 copy-done.11
  62.1 0.0 copy-done.13
  62.1 1.4 %copy.6.refs_0_ = s32[32,2]{1,0:T(8,128)} copy(s32[32,2]{0,1:T(2,128)} %param.8) | data formatting | bytes 512 | tf_op args[3]
  63.5 0.6 pad_add_fusion.refs_2_
  64.1 0.0 collective-permute-done.15.refs_21_
  64.1 0.0 collective-permute-done.12.refs_18_
  64.1 0.0 collective-permute-done.13.refs_19_
  64.1 0.0 collective-permute-done.14.refs_20_
  64.1 0.0 collective-permute-done.16.refs_22_
  64.2 43.1 %shard_map.56 = f32[8,16,16,8,128]{4,3,2,1,0:T(8,128)} custom-call(s32[32,2]{1,0:T(8,128)} %copy.6.refs_0_, s32[4]{0:T(128)} %refs_1_.1, s32[4]{0:T(128)} %pad_add_fusion.refs_2_, f32[3,2,4,24,128]{4,3,2,1,0:T(8,128)} %copy-done.11, f32[2,3,2,4,24,128]{5,4,3,2,1,0:T(8,128)} %copy-done, f32[3,2,4,80,128]{4,3,2,1,0:T(8,128)} %copy-done.4, ...), custom_call_target="tpu_custom_call" | custom-call | tf_op jit(solution)/shard_map/pallas_call | solution.py:163
  (20 shorter events, 0.1 us)
Async XLA Ops:
  0.0 1.2 %copy-start.1 = (f32[4,128,512]{2,1,0:T(8,128)S(1)}, f32[4,128,512]{2,1,0:T(8,128)}, u32[]{:S(2)}) copy-start(f32[4,128,512]{2,1,0:T(8,128)} %psi_ref.1) | copy-start | bytes 3145732
  1.2 1.2 %copy-start.2 = (f32[4,128,512]{2,1,0:T(8,128)S(1)}, f32[4,128,512]{2,1,0:T(8,128)}, u32[]{:S(2)}) copy-start(f32[4,128,512]{2,1,0:T(8,128)} %phi_ref.1) | copy-start | bytes 3145732
  2.5 1.2 %copy-start.3 = (s32[4,128,512]{2,1,0:T(8,128)S(1)}, s32[4,128,512]{2,1,0:T(8,128)}, u32[]{:S(2)}) copy-start(s32[4,128,512]{2,1,0:T(8,128)} %mask_ref.1) | copy-start | bytes 3145732
  3.9 60.2 %copy-start = (f32[2,3,2,4,24,128]{5,4,3,2,1,0:T(8,128)}, f32[2,3,2,4,24,128]{5,4,3,2,1,0:T(8,128)S(1)}, u32[]{:S(2)}) copy-start(f32[2,3,2,4,24,128]{5,4,3,2,1,0:T(8,128)S(1)} %get-tuple-element.10.refs_4_) | copy-start | bytes 1769476
  3.9 60.2 %copy-start.4 = (f32[3,2,4,80,128]{4,3,2,1,0:T(8,128)}, f32[3,2,4,80,128]{4,3,2,1,0:T(8,128)S(1)}, u32[]{:S(2)}) copy-start(f32[3,2,4,80,128]{4,3,2,1,0:T(8,128)S(1)} %get-tuple-element.13.refs_5_) | copy-start | bytes 2949124
  3.9 60.2 %copy-start.5 = (f32[2,4,128,128]{3,2,1,0:T(8,128)}, f32[2,4,128,128]{3,2,1,0:T(8,128)S(1)}, u32[]{:S(2)}) copy-start(f32[2,4,128,128]{3,2,1,0:T(8,128)S(1)} %get-tuple-element.14.refs_7_) | copy-start | bytes 1572868
  3.9 19.7 %collective-permute-start.2 = (f32[2,3,2,4,24,128]{5,4,3,2,1,0:T(8,128)S(1)}, f32[2,3,2,4,24,128]{5,4,3,2,1,0:T(8,128)S(1)}, u32[]{:S(2)}, u32[]{:S(2)}) collective-permute-start(f32[2,3,2,4,24,128]{5,4,3,2,1,0:T(8,128)S(1)} %get-tuple-element.10.refs_4_), channel_id=1, source_target_pairs={{0,2},{1,3},{2,0},{3,1},{4,6},{5,7},{6,4},{7,5},{8,10},{9,11},{10,... | collective-permute-start | bytes 1769480 | tf_op jit(solution)/shard_map/ppermute | solution.py:191
  7.0 10.4 %collective-permute-start.1 = (f32[3,2,4,24,128]{4,3,2,1,0:T(8,128)S(1)}, f32[3,2,4,24,128]{4,3,2,1,0:T(8,128)S(1)}, u32[]{:S(2)}, u32[]{:S(2)}) collective-permute-start(f32[3,2,4,24,128]{4,3,2,1,0:T(8,128)S(1)} %get-tuple-element.17), channel_id=1, source_target_pairs={{4,0},{8,4},{12,8},{16,12},{20,16},{24,20},{28,24},{5,1},{9,5},{13... | collective-permute-start | bytes 884744 | tf_op jit(solution)/shard_map/ppermute | solution.py:197
  8.3 15.3 %collective-permute-start = (f32[3,2,4,24,128]{4,3,2,1,0:T(8,128)S(1)}, f32[3,2,4,24,128]{4,3,2,1,0:T(8,128)S(1)}, u32[]{:S(2)}, u32[]{:S(2)}) collective-permute-start(f32[3,2,4,24,128]{4,3,2,1,0:T(8,128)S(1)} %get-tuple-element.18), channel_id=1, source_target_pairs={{0,4},{4,8},{8,12},{12,16},{16,20},{20,24},{24,28},{1,5},{5,9},{9,... | collective-permute-start | bytes 884744 | tf_op jit(solution)/shard_map/ppermute | solution.py:194
  17.4 44.7 %copy-start.10 = (f32[3,2,4,24,128]{4,3,2,1,0:T(8,128)}, f32[3,2,4,24,128]{4,3,2,1,0:T(8,128)S(1)}, u32[]{:S(2)}) copy-start(f32[3,2,4,24,128]{4,3,2,1,0:T(8,128)S(1)} %collective-permute-done.1.refs_6_) | copy-start | bytes 884740
  23.6 38.5 %copy-start.11 = (f32[3,2,4,24,128]{4,3,2,1,0:T(8,128)}, f32[3,2,4,24,128]{4,3,2,1,0:T(8,128)S(1)}, u32[]{:S(2)}) copy-start(f32[3,2,4,24,128]{4,3,2,1,0:T(8,128)S(1)} %collective-permute-done.refs_3_) | copy-start | bytes 884740
  23.6 40.5 %copy-start.6 = (f32[2,3,2,4,24,128]{5,4,3,2,1,0:T(8,128)}, f32[2,3,2,4,24,128]{5,4,3,2,1,0:T(8,128)S(1)}, u32[]{:S(2)}) copy-start(f32[2,3,2,4,24,128]{5,4,3,2,1,0:T(8,128)S(1)} %collective-permute-done.2.refs_9_) | copy-start | bytes 1769476
  23.6 23.8 %collective-permute-start.4 = (f32[3,2,4,80,128]{4,3,2,1,0:T(8,128)S(1)}, f32[3,2,4,80,128]{4,3,2,1,0:T(8,128)}, u32[]{:S(2)}, u32[]{:S(2)}) collective-permute-start(f32[3,2,4,80,128]{4,3,2,1,0:T(8,128)S(1)} %get-tuple-element.13.refs_5_), channel_id=1, source_target_pairs={{0,2},{1,3},{2,0},{3,1},{4,6},{5,7},{6,4},{7,5},{8,10},{9,11},{10,... | collective-permute-start | bytes 2949128 | tf_op jit(solution)/shard_map/ppermute | solution.py:191
  24.2 11.5 %collective-permute-start.5 = (f32[3,2,4,24,128]{4,3,2,1,0:T(8,128)S(1)}, f32[3,2,4,24,128]{4,3,2,1,0:T(8,128)}, u32[]{:S(2)}, u32[]{:S(2)}) collective-permute-start(f32[3,2,4,24,128]{4,3,2,1,0:T(8,128)S(1)} %get-tuple-element.15), channel_id=1, source_target_pairs={{4,0},{8,4},{12,8},{16,12},{20,16},{24,20},{28,24},{5,1},{9,5},{13... | collective-permute-start | bytes 884744 | tf_op jit(solution)/shard_map/ppermute | solution.py:197
  25.5 22.4 %collective-permute-start.11 = (f32[2,4,128,128]{3,2,1,0:T(8,128)S(1)}, f32[2,4,128,128]{3,2,1,0:T(8,128)S(1)}, u32[]{:S(2)}, u32[]{:S(2)}) collective-permute-start(f32[2,4,128,128]{3,2,1,0:T(8,128)S(1)} %get-tuple-element.14.refs_7_), channel_id=1, source_target_pairs={{0,1},{1,0},{2,3},{3,2},{4,5},{5,4},{6,7},{7,6},{8,9},{9,8},{10,11... | collective-permute-start | bytes 1572872 | tf_op jit(solution)/shard_map/ppermute | solution.py:191
  25.5 16.5 %collective-permute-start.3 = (f32[3,2,4,24,128]{4,3,2,1,0:T(8,128)S(1)}, f32[3,2,4,24,128]{4,3,2,1,0:T(8,128)}, u32[]{:S(2)}, u32[]{:S(2)}) collective-permute-start(f32[3,2,4,24,128]{4,3,2,1,0:T(8,128)S(1)} %get-tuple-element.16), channel_id=1, source_target_pairs={{0,4},{4,8},{8,12},{12,16},{16,20},{20,24},{24,28},{1,5},{5,9},{9,... | collective-permute-start | bytes 884744 | tf_op jit(solution)/shard_map/ppermute | solution.py:194
  31.3 29.7 %collective-permute-start.9 = (f32[3,2,4,80,128]{4,3,2,1,0:T(8,128)S(1)}, f32[3,2,4,80,128]{4,3,2,1,0:T(8,128)S(1)}, u32[]{:S(2)}, u32[]{:S(2)}) collective-permute-start(f32[3,2,4,80,128]{4,3,2,1,0:T(8,128)S(1)} %get-tuple-element.13.refs_5_), channel_id=1, source_target_pairs={{0,1},{1,0},{2,3},{3,2},{4,5},{5,4},{6,7},{7,6},{8,9},{9,8},{10,11... | collective-permute-start | bytes 2949128 | tf_op jit(solution)/shard_map/ppermute | solution.py:191
  35.6 12.8 %collective-permute-start.10 = (f32[3,2,4,24,128]{4,3,2,1,0:T(8,128)S(1)}, f32[3,2,4,24,128]{4,3,2,1,0:T(8,128)S(1)}, u32[]{:S(2)}, u32[]{:S(2)}) collective-permute-start(f32[3,2,4,24,128]{4,3,2,1,0:T(8,128)S(1)} %collective-permute-done.1.refs_6_), channel_id=1, source_target_pairs={{0,1},{1,0},{2,3},{3,2},{4,5},{5,4},{6,7},{7,6},{8,9},{9,8},{10,11... | collective-permute-start | bytes 884744 | tf_op jit(solution)/shard_map/ppermute | solution.py:191
  47.4 13.1 %collective-permute-start.6 = (f32[2,4,128,128]{3,2,1,0:T(8,128)S(1)}, f32[2,4,128,128]{3,2,1,0:T(8,128)}, u32[]{:S(2)}, u32[]{:S(2)}) collective-permute-start(f32[2,4,128,128]{3,2,1,0:T(8,128)S(1)} %get-tuple-element.14.refs_7_), channel_id=1, source_target_pairs={{0,2},{1,3},{2,0},{3,1},{4,6},{5,7},{6,4},{7,5},{8,10},{9,11},{10,... | collective-permute-start | bytes 1572872 | tf_op jit(solution)/shard_map/ppermute | solution.py:191
  47.9 16.2 %collective-permute-start.14 = (f32[3,2,4,80,128]{4,3,2,1,0:T(8,128)}, f32[3,2,4,80,128]{4,3,2,1,0:T(8,128)}, u32[]{:S(2)}, u32[]{:S(2)}) collective-permute-start(f32[3,2,4,80,128]{4,3,2,1,0:T(8,128)} %collective-permute-done.4.refs_10_), channel_id=1, source_target_pairs={{0,1},{1,0},{2,3},{3,2},{4,5},{5,4},{6,7},{7,6},{8,9},{9,8},{10,11... | collective-permute-start | bytes 2949128 | tf_op jit(solution)/shard_map/ppermute | solution.py:191
  47.9 14.2 %copy-start.9 = (f32[2,4,128,128]{3,2,1,0:T(8,128)}, f32[2,4,128,128]{3,2,1,0:T(8,128)S(1)}, u32[]{:S(2)}) copy-start(f32[2,4,128,128]{3,2,1,0:T(8,128)S(1)} %collective-permute-done.11.refs_17_) | copy-start | bytes 1572868
  47.9 12.6 %collective-permute-start.8 = (f32[2,3,2,4,24,128]{5,4,3,2,1,0:T(8,128)S(1)}, f32[2,3,2,4,24,128]{5,4,3,2,1,0:T(8,128)S(1)}, u32[]{:S(2)}, u32[]{:S(2)}) collective-permute-start(f32[2,3,2,4,24,128]{5,4,3,2,1,0:T(8,128)S(1)} %get-tuple-element.10.refs_4_), channel_id=1, source_target_pairs={{0,1},{1,0},{2,3},{3,2},{4,5},{5,4},{6,7},{7,6},{8,9},{9,8},{10,11... | collective-permute-start | bytes 1769480 | tf_op jit(solution)/shard_map/ppermute | solution.py:191
  48.4 13.7 %copy-start.12 = (f32[3,2,4,24,128]{4,3,2,1,0:T(8,128)}, f32[3,2,4,24,128]{4,3,2,1,0:T(8,128)S(1)}, u32[]{:S(2)}) copy-start(f32[3,2,4,24,128]{4,3,2,1,0:T(8,128)S(1)} %collective-permute-done.10.refs_16_) | copy-start | bytes 884740
  48.4 3.3 %collective-permute-start.7 = (f32[3,2,4,24,128]{4,3,2,1,0:T(8,128)S(1)}, f32[3,2,4,24,128]{4,3,2,1,0:T(8,128)S(1)}, u32[]{:S(2)}, u32[]{:S(2)}) collective-permute-start(f32[3,2,4,24,128]{4,3,2,1,0:T(8,128)S(1)} %collective-permute-done.refs_3_), channel_id=1, source_target_pairs={{0,1},{1,0},{2,3},{3,2},{4,5},{5,4},{6,7},{7,6},{8,9},{9,8},{10,11... | collective-permute-start | bytes 884744 | tf_op jit(solution)/shard_map/ppermute | solution.py:191
  51.7 10.4 %copy-start.13 = (f32[3,2,4,24,128]{4,3,2,1,0:T(8,128)}, f32[3,2,4,24,128]{4,3,2,1,0:T(8,128)S(1)}, u32[]{:S(2)}) copy-start(f32[3,2,4,24,128]{4,3,2,1,0:T(8,128)S(1)} %collective-permute-done.7.refs_13_) | copy-start | bytes 884740
  51.7 12.4 %collective-permute-start.13 = (f32[2,3,2,4,24,128]{5,4,3,2,1,0:T(8,128)S(1)}, f32[2,3,2,4,24,128]{5,4,3,2,1,0:T(8,128)}, u32[]{:S(2)}, u32[]{:S(2)}) collective-permute-start(f32[2,3,2,4,24,128]{5,4,3,2,1,0:T(8,128)S(1)} %collective-permute-done.2.refs_9_), channel_id=1, source_target_pairs={{0,1},{1,0},{2,3},{3,2},{4,5},{5,4},{6,7},{7,6},{8,9},{9,8},{10,11... | collective-permute-start | bytes 1769480 | tf_op jit(solution)/shard_map/ppermute | solution.py:191
  60.5 3.6 %collective-permute-start.16 = (f32[2,4,128,128]{3,2,1,0:T(8,128)}, f32[2,4,128,128]{3,2,1,0:T(8,128)}, u32[]{:S(2)}, u32[]{:S(2)}) collective-permute-start(f32[2,4,128,128]{3,2,1,0:T(8,128)} %collective-permute-done.6.refs_12_), channel_id=1, source_target_pairs={{0,1},{1,0},{2,3},{3,2},{4,5},{5,4},{6,7},{7,6},{8,9},{9,8},{10,11... | collective-permute-start | bytes 1572872 | tf_op jit(solution)/shard_map/ppermute | solution.py:191
  60.5 3.7 %copy-start.8 = (f32[2,3,2,4,24,128]{5,4,3,2,1,0:T(8,128)}, f32[2,3,2,4,24,128]{5,4,3,2,1,0:T(8,128)S(1)}, u32[]{:S(2)}) copy-start(f32[2,3,2,4,24,128]{5,4,3,2,1,0:T(8,128)S(1)} %collective-permute-done.8.refs_14_) | copy-start | bytes 1769476
  60.5 3.6 %collective-permute-start.15 = (f32[3,2,4,24,128]{4,3,2,1,0:T(8,128)}, f32[3,2,4,24,128]{4,3,2,1,0:T(8,128)}, u32[]{:S(2)}, u32[]{:S(2)}) collective-permute-start(f32[3,2,4,24,128]{4,3,2,1,0:T(8,128)} %collective-permute-done.5.refs_11_), channel_id=1, source_target_pairs={{0,1},{1,0},{2,3},{3,2},{4,5},{5,4},{6,7},{7,6},{8,9},{9,8},{10,11... | collective-permute-start | bytes 884744 | tf_op jit(solution)/shard_map/ppermute | solution.py:191
  61.0 1.0 copy-start.7
  62.0 2.1 %collective-permute-start.12 = (f32[3,2,4,24,128]{4,3,2,1,0:T(8,128)}, f32[3,2,4,24,128]{4,3,2,1,0:T(8,128)}, u32[]{:S(2)}, u32[]{:S(2)}) collective-permute-start(f32[3,2,4,24,128]{4,3,2,1,0:T(8,128)} %collective-permute-done.3.refs_8_), channel_id=1, source_target_pairs={{0,1},{1,0},{2,3},{3,2},{4,5},{5,4},{6,7},{7,6},{8,9},{9,8},{10,11... | collective-permute-start | bytes 884744 | tf_op jit(solution)/shard_map/ppermute | solution.py:191

commit v4 on v3

--- a/solution.py
+++ b/solution.py
@@ -199,14 +199,14 @@
     far = [2 * k for k in range(1, count // 2)]
     above, below = from_rows_above(edges[1]), from_rows_below(edges[0])
     far_edges = [edges] + [swap(edges, bits) for bits in far]
-    sent = after(mid, far_edges[-1], above, below)
-    far_mid = [mid] + [swap(sent, bits) for bits in far]
+    far_mid = [mid] + [swap(mid, bits) for bits in far]
+    sent = after(first, far_edges[-1], above, below)
+    far_first = [first] + [swap(sent, bits) for bits in far]
     above, below = [above], [below]
     for value in far_edges[1:]:
         above.append(from_rows_above(value[1]))
         below.append(from_rows_below(value[0]))
-    sent = after(first, far_mid[-1], above[-1], below[-1])
-    far_first = [first] + [swap(sent, bits) for bits in far]
+    far_mid = [mid] + [after(value, above[-1], below[-1]) for value in far_mid[1:]]
     pieces, owners = [], []
     for k in range(count // 2):
         pieces.append((above[k], far_edges[k], far_mid[k], below[k], far_first[k]))

time: 108 us -> 100 us (0.926)
  waiting for transfers between devices: 38.5 us -> 30.6 us
    ppermute x2, waiting for transfers between devices: 12.6 us -> 6.04 us  [from_rows_above(): return lax.ppermute(value, 'sky', [(i, i + 1) for i in range(skies - 1)])]
    ppermute x2, waiting for transfers between devices: 8.58 us -> 2.5 us  [from_rows_below(): return lax.ppermute(value, 'sky', [(i + 1, i) for i in range(skies - 1)])]
    ppermute x13, waiting for transfers between devices: 17.3 us -> 22 us  [swap(): return lax.ppermute(value, 'vel', [(i, i ^ bits) for i in range(count)])]
  transfers between devices with their start and end apart: 17 -> 17, of which waited for: 7 -> 6; matrix products, arithmetic and copies ran while one was open for 2% -> 2% of each run, Pallas kernels for 0% -> 0%
where the time goes in v4:
time: 100 us; the launch traced here: 99.6 us
  Pallas kernels  43.5 us (44%)
  waiting for transfers between devices  30.6 us (31%)
  starting transfers between devices  18.7 us (19%)
  local copies, waits for them, and re-layouts  6.11 us (6%)
    pallas_call x1, Pallas kernels, stack(): pl.pallas_call(functools.partial(stack_kernel, count, tiles, later, rows,...  43.2 us
    ppermute x13, waiting for transfers between devices, swap(): return lax.ppermute(value, 'vel', [(i, i ^ bits) for i in range(count)])  22 us
    ppermute x2, starting transfers between devices, from_rows_above(): return lax.ppermute(value, 'sky', [(i, i + 1) for i in range(skies - 1)])  9.84 us
    ppermute x13, starting transfers between devices, swap(): return lax.ppermute(value, 'vel', [(i, i ^ bits) for i in range(count)])  6.27 us
    ppermute x2, waiting for transfers between devices, from_rows_above(): return lax.ppermute(value, 'sky', [(i, i + 1) for i in range(skies - 1)])  6.04 us
    unnamed x29, local copies, waits for them, and re-layouts  6.03 us
    ppermute x2, starting transfers between devices, from_rows_below(): return lax.ppermute(value, 'sky', [(i + 1, i) for i in range(skies - 1)])  2.58 us
    ppermute x2, waiting for transfers between devices, from_rows_below(): return lax.ppermute(value, 'sky', [(i + 1, i) for i in range(skies - 1)])  2.5 us
  transfers between devices with their start and end apart: 17, of which 6 were waited for; matrix products, arithmetic and copies ran while one was open for 2% of the time, Pallas kernels for 0%

profile of v4, /device:TPU:0, one launch (start us, length us, event | category | flops | bytes accessed | tf_op | source)
XLA Modules:
  0.0 99.6 jit_solution(9888179241614348422)
XLA Ops:
  0.0 1.2 %copy-done.1 = f32[4,128,512]{2,1,0:T(8,128)S(1)} copy-done((f32[4,128,512]{2,1,0:T(8,128)S(1)}, f32[4,128,512]{2,1,0:T(8,128)}, u32[]{:S(2)}) %copy-start.1) | copy-done | bytes 1048600
  1.2 1.2 %copy-done.2 = f32[4,128,512]{2,1,0:T(8,128)S(1)} copy-done((f32[4,128,512]{2,1,0:T(8,128)S(1)}, f32[4,128,512]{2,1,0:T(8,128)}, u32[]{:S(2)}) %copy-start.2) | copy-done | bytes 1048600
  2.5 1.2 %copy-done.3 = s32[4,128,512]{2,1,0:T(8,128)S(1)} copy-done((s32[4,128,512]{2,1,0:T(8,128)S(1)}, s32[4,128,512]{2,1,0:T(8,128)}, u32[]{:S(2)}) %copy-start.3) | copy-done | bytes 1048600
  3.7 0.2 shard_map.55
  3.9 0.0 copy-start
  3.9 0.0 copy-start.4
  3.9 0.0 copy-start.5
  3.9 3.0 %collective-permute-start.2 = (f32[2,3,2,4,24,128]{5,4,3,2,1,0:T(8,128)S(1)}, f32[2,3,2,4,24,128]{5,4,3,2,1,0:T(8,128)S(1)}, u32[]{:S(2)}, u32[]{:S(2)}) collective-permute-start(f32[2,3,2,4,24,128]{5,4,3,2,1,0:T(8,128)S(1)} %get-tuple-element.10.refs_4_), channel_id=1, source_target_pairs={{0,2},{1,3},{2,0},{3,1},{4,6},{5,7},{6,4},{7,5},{8,10},{9,11},{10,... | collective-permute-start | bytes 1769480 | tf_op jit(solution)/shard_map/ppermute | solution.py:191
  7.0 0.1 collective-permute-start.4
  7.1 1.3 %collective-permute-start.1 = (f32[3,2,4,24,128]{4,3,2,1,0:T(8,128)S(1)}, f32[3,2,4,24,128]{4,3,2,1,0:T(8,128)S(1)}, u32[]{:S(2)}, u32[]{:S(2)}) collective-permute-start(f32[3,2,4,24,128]{4,3,2,1,0:T(8,128)S(1)} %get-tuple-element.17), channel_id=1, source_target_pairs={{4,0},{8,4},{12,8},{16,12},{20,16},{24,20},{28,24},{5,1},{9,5},{13... | collective-permute-start | bytes 884744 | tf_op jit(solution)/shard_map/ppermute | solution.py:197
  8.4 4.6 %collective-permute-start = (f32[3,2,4,24,128]{4,3,2,1,0:T(8,128)S(1)}, f32[3,2,4,24,128]{4,3,2,1,0:T(8,128)S(1)}, u32[]{:S(2)}, u32[]{:S(2)}) collective-permute-start(f32[3,2,4,24,128]{4,3,2,1,0:T(8,128)S(1)} %get-tuple-element.18), channel_id=1, source_target_pairs={{0,4},{4,8},{8,12},{12,16},{16,20},{20,24},{24,28},{1,5},{5,9},{9,... | collective-permute-start | bytes 884744 | tf_op jit(solution)/shard_map/ppermute | solution.py:194
  13.0 8.2 %collective-permute-done.2.refs_9_ = f32[2,3,2,4,24,128]{5,4,3,2,1,0:T(8,128)S(1)} collective-permute-done((f32[2,3,2,4,24,128]{5,4,3,2,1,0:T(8,128)S(1)}, f32[2,3,2,4,24,128]{5,4,3,2,1,0:T(8,128)S(1)}, u32[]{:S(2)}, u32[]{:S(2)}) %collective-permute-start.2) | collective-permute-done | bytes 589856 | tf_op jit(solution)/shard_map/ppermute | solution.py:191
  21.2 1.3 %collective-permute-start.5 = (f32[3,2,4,24,128]{4,3,2,1,0:T(8,128)S(1)}, f32[3,2,4,24,128]{4,3,2,1,0:T(8,128)}, u32[]{:S(2)}, u32[]{:S(2)}) collective-permute-start(f32[3,2,4,24,128]{4,3,2,1,0:T(8,128)S(1)} %get-tuple-element.15), channel_id=1, source_target_pairs={{4,0},{8,4},{12,8},{16,12},{20,16},{24,20},{28,24},{5,1},{9,5},{13... | collective-permute-start | bytes 884744 | tf_op jit(solution)/shard_map/ppermute | solution.py:197
  22.5 0.1 collective-permute-start.11
  22.6 0.0 collective-permute-done.1.refs_6_
  22.6 0.0 copy-start.10
  22.6 5.3 %collective-permute-start.3 = (f32[3,2,4,24,128]{4,3,2,1,0:T(8,128)S(1)}, f32[3,2,4,24,128]{4,3,2,1,0:T(8,128)}, u32[]{:S(2)}, u32[]{:S(2)}) collective-permute-start(f32[3,2,4,24,128]{4,3,2,1,0:T(8,128)S(1)} %get-tuple-element.16), channel_id=1, source_target_pairs={{0,4},{4,8},{8,12},{12,16},{16,20},{20,24},{24,28},{1,5},{5,9},{9,... | collective-permute-start | bytes 884744 | tf_op jit(solution)/shard_map/ppermute | solution.py:194
  27.8 0.0 collective-permute-done.refs_3_
  27.8 0.2 collective-permute-start.9
  28.0 2.5 %collective-permute-done.5.refs_11_ = f32[3,2,4,24,128]{4,3,2,1,0:T(8,128)} collective-permute-done((f32[3,2,4,24,128]{4,3,2,1,0:T(8,128)S(1)}, f32[3,2,4,24,128]{4,3,2,1,0:T(8,128)}, u32[]{:S(2)}, u32[]{:S(2)}) %collective-permute-start.5) | collective-permute-done | bytes 294944 | tf_op jit(solution)/shard_map/ppermute | solution.py:197
  30.5 0.0 collective-permute-start.10
  30.5 6.0 %collective-permute-done.3.refs_8_ = f32[3,2,4,24,128]{4,3,2,1,0:T(8,128)} collective-permute-done((f32[3,2,4,24,128]{4,3,2,1,0:T(8,128)S(1)}, f32[3,2,4,24,128]{4,3,2,1,0:T(8,128)}, u32[]{:S(2)}, u32[]{:S(2)}) %collective-permute-start.3) | collective-permute-done | bytes 294944 | tf_op jit(solution)/shard_map/ppermute | solution.py:194
  36.6 1.5 %collective-permute-start.6 = (f32[2,4,128,128]{3,2,1,0:T(8,128)S(1)}, f32[2,4,128,128]{3,2,1,0:T(8,128)}, u32[]{:S(2)}, u32[]{:S(2)}) collective-permute-start(f32[2,4,128,128]{3,2,1,0:T(8,128)S(1)} %get-tuple-element.14.refs_7_), channel_id=1, source_target_pairs={{0,2},{1,3},{2,0},{3,1},{4,6},{5,7},{6,4},{7,5},{8,10},{9,11},{10,... | collective-permute-start | bytes 1572872 | tf_op jit(solution)/shard_map/ppermute | solution.py:191
  38.1 4.2 %collective-permute-done.4.refs_10_ = f32[3,2,4,80,128]{4,3,2,1,0:T(8,128)} collective-permute-done((f32[3,2,4,80,128]{4,3,2,1,0:T(8,128)S(1)}, f32[3,2,4,80,128]{4,3,2,1,0:T(8,128)}, u32[]{:S(2)}, u32[]{:S(2)}) %collective-permute-start.4) | collective-permute-done | bytes 983072 | tf_op jit(solution)/shard_map/ppermute | solution.py:191
  42.3 0.0 collective-permute-start.14
  42.3 0.0 collective-permute-done.11.refs_17_
  42.3 0.5 collective-permute-start.8
  42.8 0.0 collective-permute-done.10.refs_16_
  42.8 0.1 collective-permute-start.7
  42.9 3.2 %collective-permute-done.7.refs_13_ = f32[3,2,4,24,128]{4,3,2,1,0:T(8,128)S(1)} collective-permute-done((f32[3,2,4,24,128]{4,3,2,1,0:T(8,128)S(1)}, f32[3,2,4,24,128]{4,3,2,1,0:T(8,128)S(1)}, u32[]{:S(2)}, u32[]{:S(2)}) %collective-permute-start.7) | collective-permute-done | bytes 294944 | tf_op jit(solution)/shard_map/ppermute | solution.py:191
  46.1 0.1 collective-permute-start.13
  46.3 6.4 %collective-permute-done.6.refs_12_ = f32[2,4,128,128]{3,2,1,0:T(8,128)} collective-permute-done((f32[2,4,128,128]{3,2,1,0:T(8,128)S(1)}, f32[2,4,128,128]{3,2,1,0:T(8,128)}, u32[]{:S(2)}, u32[]{:S(2)}) %collective-permute-start.6) | collective-permute-done | bytes 524320 | tf_op jit(solution)/shard_map/ppermute | solution.py:191
  52.7 0.0 collective-permute-start.16
  52.7 0.0 collective-permute-done.8.refs_14_
  52.7 0.5 collective-permute-start.15
  53.2 0.0 collective-permute-done.9.refs_15_
  53.2 1.0 copy-done.7
  54.2 0.1 collective-permute-start.12
  54.3 0.0 copy-done.12
  54.3 0.0 copy-done.13
  54.3 1.4 %copy.6.refs_0_ = s32[32,2]{1,0:T(8,128)} copy(s32[32,2]{0,1:T(2,128)} %param.8) | data formatting | bytes 512 | tf_op args[3]
  55.7 0.6 pad_add_fusion.refs_2_
  56.3 0.0 collective-permute-done.15.refs_21_
  56.3 0.0 collective-permute-done.12.refs_18_
  56.3 0.0 collective-permute-done.13.refs_19_
  56.3 0.0 collective-permute-done.16.refs_22_
  56.3 0.0 collective-permute-done.14.refs_20_
  56.4 43.2 %shard_map.56 = f32[8,16,16,8,128]{4,3,2,1,0:T(8,128)} custom-call(s32[32,2]{1,0:T(8,128)} %copy.6.refs_0_, s32[4]{0:T(128)} %refs_1_.1, s32[4]{0:T(128)} %pad_add_fusion.refs_2_, f32[3,2,4,24,128]{4,3,2,1,0:T(8,128)} %copy-done.11, f32[2,3,2,4,24,128]{5,4,3,2,1,0:T(8,128)} %copy-done, f32[3,2,4,80,128]{4,3,2,1,0:T(8,128)} %copy-done.4, ...), custom_call_target="tpu_custom_call" | custom-call | tf_op jit(solution)/shard_map/pallas_call | solution.py:163
  (20 shorter events, 0.1 us)
Async XLA Ops:
  0.0 1.2 %copy-start.1 = (f32[4,128,512]{2,1,0:T(8,128)S(1)}, f32[4,128,512]{2,1,0:T(8,128)}, u32[]{:S(2)}) copy-start(f32[4,128,512]{2,1,0:T(8,128)} %psi_ref.1) | copy-start | bytes 3145732
  1.2 1.2 %copy-start.2 = (f32[4,128,512]{2,1,0:T(8,128)S(1)}, f32[4,128,512]{2,1,0:T(8,128)}, u32[]{:S(2)}) copy-start(f32[4,128,512]{2,1,0:T(8,128)} %phi_ref.1) | copy-start | bytes 3145732
  2.5 1.2 %copy-start.3 = (s32[4,128,512]{2,1,0:T(8,128)S(1)}, s32[4,128,512]{2,1,0:T(8,128)}, u32[]{:S(2)}) copy-start(s32[4,128,512]{2,1,0:T(8,128)} %mask_ref.1) | copy-start | bytes 3145732
  3.9 52.4 %copy-start = (f32[2,3,2,4,24,128]{5,4,3,2,1,0:T(8,128)}, f32[2,3,2,4,24,128]{5,4,3,2,1,0:T(8,128)S(1)}, u32[]{:S(2)}) copy-start(f32[2,3,2,4,24,128]{5,4,3,2,1,0:T(8,128)S(1)} %get-tuple-element.10.refs_4_) | copy-start | bytes 1769476
  3.9 52.4 %copy-start.4 = (f32[3,2,4,80,128]{4,3,2,1,0:T(8,128)}, f32[3,2,4,80,128]{4,3,2,1,0:T(8,128)S(1)}, u32[]{:S(2)}) copy-start(f32[3,2,4,80,128]{4,3,2,1,0:T(8,128)S(1)} %get-tuple-element.11.refs_5_) | copy-start | bytes 2949124
  3.9 52.4 %copy-start.5 = (f32[2,4,128,128]{3,2,1,0:T(8,128)}, f32[2,4,128,128]{3,2,1,0:T(8,128)S(1)}, u32[]{:S(2)}) copy-start(f32[2,4,128,128]{3,2,1,0:T(8,128)S(1)} %get-tuple-element.14.refs_7_) | copy-start | bytes 1572868
  3.9 17.2 %collective-permute-start.2 = (f32[2,3,2,4,24,128]{5,4,3,2,1,0:T(8,128)S(1)}, f32[2,3,2,4,24,128]{5,4,3,2,1,0:T(8,128)S(1)}, u32[]{:S(2)}, u32[]{:S(2)}) collective-permute-start(f32[2,3,2,4,24,128]{5,4,3,2,1,0:T(8,128)S(1)} %get-tuple-element.10.refs_4_), channel_id=1, source_target_pairs={{0,2},{1,3},{2,0},{3,1},{4,6},{5,7},{6,4},{7,5},{8,10},{9,11},{10,... | collective-permute-start | bytes 1769480 | tf_op jit(solution)/shard_map/ppermute | solution.py:191
  7.0 35.3 %collective-permute-start.4 = (f32[3,2,4,80,128]{4,3,2,1,0:T(8,128)S(1)}, f32[3,2,4,80,128]{4,3,2,1,0:T(8,128)}, u32[]{:S(2)}, u32[]{:S(2)}) collective-permute-start(f32[3,2,4,80,128]{4,3,2,1,0:T(8,128)S(1)} %get-tuple-element.11.refs_5_), channel_id=1, source_target_pairs={{0,2},{1,3},{2,0},{3,1},{4,6},{5,7},{6,4},{7,5},{8,10},{9,11},{10,... | collective-permute-start | bytes 2949128 | tf_op jit(solution)/shard_map/ppermute | solution.py:191
  7.1 15.5 %collective-permute-start.1 = (f32[3,2,4,24,128]{4,3,2,1,0:T(8,128)S(1)}, f32[3,2,4,24,128]{4,3,2,1,0:T(8,128)S(1)}, u32[]{:S(2)}, u32[]{:S(2)}) collective-permute-start(f32[3,2,4,24,128]{4,3,2,1,0:T(8,128)S(1)} %get-tuple-element.17), channel_id=1, source_target_pairs={{4,0},{8,4},{12,8},{16,12},{20,16},{24,20},{28,24},{5,1},{9,5},{13... | collective-permute-start | bytes 884744 | tf_op jit(solution)/shard_map/ppermute | solution.py:197
  8.4 19.5 %collective-permute-start = (f32[3,2,4,24,128]{4,3,2,1,0:T(8,128)S(1)}, f32[3,2,4,24,128]{4,3,2,1,0:T(8,128)S(1)}, u32[]{:S(2)}, u32[]{:S(2)}) collective-permute-start(f32[3,2,4,24,128]{4,3,2,1,0:T(8,128)S(1)} %get-tuple-element.18), channel_id=1, source_target_pairs={{0,4},{4,8},{8,12},{12,16},{16,20},{20,24},{24,28},{1,5},{5,9},{9,... | collective-permute-start | bytes 884744 | tf_op jit(solution)/shard_map/ppermute | solution.py:194
  21.1 35.2 %copy-start.6 = (f32[2,3,2,4,24,128]{5,4,3,2,1,0:T(8,128)}, f32[2,3,2,4,24,128]{5,4,3,2,1,0:T(8,128)S(1)}, u32[]{:S(2)}) copy-start(f32[2,3,2,4,24,128]{5,4,3,2,1,0:T(8,128)S(1)} %collective-permute-done.2.refs_9_) | copy-start | bytes 1769476
  21.2 9.4 %collective-permute-start.5 = (f32[3,2,4,24,128]{4,3,2,1,0:T(8,128)S(1)}, f32[3,2,4,24,128]{4,3,2,1,0:T(8,128)}, u32[]{:S(2)}, u32[]{:S(2)}) collective-permute-start(f32[3,2,4,24,128]{4,3,2,1,0:T(8,128)S(1)} %get-tuple-element.15), channel_id=1, source_target_pairs={{4,0},{8,4},{12,8},{16,12},{20,16},{24,20},{28,24},{5,1},{9,5},{13... | collective-permute-start | bytes 884744 | tf_op jit(solution)/shard_map/ppermute | solution.py:197
  22.5 19.8 %collective-permute-start.11 = (f32[2,4,128,128]{3,2,1,0:T(8,128)S(1)}, f32[2,4,128,128]{3,2,1,0:T(8,128)S(1)}, u32[]{:S(2)}, u32[]{:S(2)}) collective-permute-start(f32[2,4,128,128]{3,2,1,0:T(8,128)S(1)} %get-tuple-element.14.refs_7_), channel_id=1, source_target_pairs={{0,1},{1,0},{2,3},{3,2},{4,5},{5,4},{6,7},{7,6},{8,9},{9,8},{10,11... | collective-permute-start | bytes 1572872 | tf_op jit(solution)/shard_map/ppermute | solution.py:191
  22.6 31.8 %copy-start.10 = (f32[3,2,4,24,128]{4,3,2,1,0:T(8,128)}, f32[3,2,4,24,128]{4,3,2,1,0:T(8,128)S(1)}, u32[]{:S(2)}) copy-start(f32[3,2,4,24,128]{4,3,2,1,0:T(8,128)S(1)} %collective-permute-done.1.refs_6_) | copy-start | bytes 884740
  22.6 14.0 %collective-permute-start.3 = (f32[3,2,4,24,128]{4,3,2,1,0:T(8,128)S(1)}, f32[3,2,4,24,128]{4,3,2,1,0:T(8,128)}, u32[]{:S(2)}, u32[]{:S(2)}) collective-permute-start(f32[3,2,4,24,128]{4,3,2,1,0:T(8,128)S(1)} %get-tuple-element.16), channel_id=1, source_target_pairs={{0,4},{4,8},{8,12},{12,16},{16,20},{20,24},{24,28},{1,5},{5,9},{9,... | collective-permute-start | bytes 884744 | tf_op jit(solution)/shard_map/ppermute | solution.py:194
  27.8 26.5 %copy-start.11 = (f32[3,2,4,24,128]{4,3,2,1,0:T(8,128)}, f32[3,2,4,24,128]{4,3,2,1,0:T(8,128)S(1)}, u32[]{:S(2)}) copy-start(f32[3,2,4,24,128]{4,3,2,1,0:T(8,128)S(1)} %collective-permute-done.refs_3_) | copy-start | bytes 884740
  27.8 25.4 %collective-permute-start.9 = (f32[3,2,4,80,128]{4,3,2,1,0:T(8,128)S(1)}, f32[3,2,4,80,128]{4,3,2,1,0:T(8,128)S(1)}, u32[]{:S(2)}, u32[]{:S(2)}) collective-permute-start(f32[3,2,4,80,128]{4,3,2,1,0:T(8,128)S(1)} %get-tuple-element.11.refs_5_), channel_id=1, source_target_pairs={{0,1},{1,0},{2,3},{3,2},{4,5},{5,4},{6,7},{7,6},{8,9},{9,8},{10,11... | collective-permute-start | bytes 2949128 | tf_op jit(solution)/shard_map/ppermute | solution.py:191
  30.5 12.3 %collective-permute-start.10 = (f32[3,2,4,24,128]{4,3,2,1,0:T(8,128)S(1)}, f32[3,2,4,24,128]{4,3,2,1,0:T(8,128)S(1)}, u32[]{:S(2)}, u32[]{:S(2)}) collective-permute-start(f32[3,2,4,24,128]{4,3,2,1,0:T(8,128)S(1)} %collective-permute-done.1.refs_6_), channel_id=1, source_target_pairs={{0,1},{1,0},{2,3},{3,2},{4,5},{5,4},{6,7},{7,6},{8,9},{9,8},{10,11... | collective-permute-start | bytes 884744 | tf_op jit(solution)/shard_map/ppermute | solution.py:191
  36.6 16.1 %collective-permute-start.6 = (f32[2,4,128,128]{3,2,1,0:T(8,128)S(1)}, f32[2,4,128,128]{3,2,1,0:T(8,128)}, u32[]{:S(2)}, u32[]{:S(2)}) collective-permute-start(f32[2,4,128,128]{3,2,1,0:T(8,128)S(1)} %get-tuple-element.14.refs_7_), channel_id=1, source_target_pairs={{0,2},{1,3},{2,0},{3,1},{4,6},{5,7},{6,4},{7,5},{8,10},{9,11},{10,... | collective-permute-start | bytes 1572872 | tf_op jit(solution)/shard_map/ppermute | solution.py:191
  42.3 14.0 %collective-permute-start.14 = (f32[3,2,4,80,128]{4,3,2,1,0:T(8,128)}, f32[3,2,4,80,128]{4,3,2,1,0:T(8,128)}, u32[]{:S(2)}, u32[]{:S(2)}) collective-permute-start(f32[3,2,4,80,128]{4,3,2,1,0:T(8,128)} %collective-permute-done.4.refs_10_), channel_id=1, source_target_pairs={{0,1},{1,0},{2,3},{3,2},{4,5},{5,4},{6,7},{7,6},{8,9},{9,8},{10,11... | collective-permute-start | bytes 2949128 | tf_op jit(solution)/shard_map/ppermute | solution.py:191
  42.3 12.0 %copy-start.9 = (f32[2,4,128,128]{3,2,1,0:T(8,128)}, f32[2,4,128,128]{3,2,1,0:T(8,128)S(1)}, u32[]{:S(2)}) copy-start(f32[2,4,128,128]{3,2,1,0:T(8,128)S(1)} %collective-permute-done.11.refs_17_) | copy-start | bytes 1572868
  42.3 10.4 %collective-permute-start.8 = (f32[2,3,2,4,24,128]{5,4,3,2,1,0:T(8,128)S(1)}, f32[2,3,2,4,24,128]{5,4,3,2,1,0:T(8,128)S(1)}, u32[]{:S(2)}, u32[]{:S(2)}) collective-permute-start(f32[2,3,2,4,24,128]{5,4,3,2,1,0:T(8,128)S(1)} %get-tuple-element.10.refs_4_), channel_id=1, source_target_pairs={{0,1},{1,0},{2,3},{3,2},{4,5},{5,4},{6,7},{7,6},{8,9},{9,8},{10,11... | collective-permute-start | bytes 1769480 | tf_op jit(solution)/shard_map/ppermute | solution.py:191
  42.8 11.5 %copy-start.12 = (f32[3,2,4,24,128]{4,3,2,1,0:T(8,128)}, f32[3,2,4,24,128]{4,3,2,1,0:T(8,128)S(1)}, u32[]{:S(2)}) copy-start(f32[3,2,4,24,128]{4,3,2,1,0:T(8,128)S(1)} %collective-permute-done.10.refs_16_) | copy-start | bytes 884740
  42.8 3.3 %collective-permute-start.7 = (f32[3,2,4,24,128]{4,3,2,1,0:T(8,128)S(1)}, f32[3,2,4,24,128]{4,3,2,1,0:T(8,128)S(1)}, u32[]{:S(2)}, u32[]{:S(2)}) collective-permute-start(f32[3,2,4,24,128]{4,3,2,1,0:T(8,128)S(1)} %collective-permute-done.refs_3_), channel_id=1, source_target_pairs={{0,1},{1,0},{2,3},{3,2},{4,5},{5,4},{6,7},{7,6},{8,9},{9,8},{10,11... | collective-permute-start | bytes 884744 | tf_op jit(solution)/shard_map/ppermute | solution.py:191
  46.1 8.2 %copy-start.13 = (f32[3,2,4,24,128]{4,3,2,1,0:T(8,128)}, f32[3,2,4,24,128]{4,3,2,1,0:T(8,128)S(1)}, u32[]{:S(2)}) copy-start(f32[3,2,4,24,128]{4,3,2,1,0:T(8,128)S(1)} %collective-permute-done.7.refs_13_) | copy-start | bytes 884740
  46.1 10.2 %collective-permute-start.13 = (f32[2,3,2,4,24,128]{5,4,3,2,1,0:T(8,128)S(1)}, f32[2,3,2,4,24,128]{5,4,3,2,1,0:T(8,128)}, u32[]{:S(2)}, u32[]{:S(2)}) collective-permute-start(f32[2,3,2,4,24,128]{5,4,3,2,1,0:T(8,128)S(1)} %collective-permute-done.2.refs_9_), channel_id=1, source_target_pairs={{0,1},{1,0},{2,3},{3,2},{4,5},{5,4},{6,7},{7,6},{8,9},{9,8},{10,11... | collective-permute-start | bytes 1769480 | tf_op jit(solution)/shard_map/ppermute | solution.py:191
  52.7 3.6 %collective-permute-start.16 = (f32[2,4,128,128]{3,2,1,0:T(8,128)}, f32[2,4,128,128]{3,2,1,0:T(8,128)}, u32[]{:S(2)}, u32[]{:S(2)}) collective-permute-start(f32[2,4,128,128]{3,2,1,0:T(8,128)} %collective-permute-done.6.refs_12_), channel_id=1, source_target_pairs={{0,1},{1,0},{2,3},{3,2},{4,5},{5,4},{6,7},{7,6},{8,9},{9,8},{10,11... | collective-permute-start | bytes 1572872 | tf_op jit(solution)/shard_map/ppermute | solution.py:191
  52.7 3.7 %copy-start.8 = (f32[2,3,2,4,24,128]{5,4,3,2,1,0:T(8,128)}, f32[2,3,2,4,24,128]{5,4,3,2,1,0:T(8,128)S(1)}, u32[]{:S(2)}) copy-start(f32[2,3,2,4,24,128]{5,4,3,2,1,0:T(8,128)S(1)} %collective-permute-done.8.refs_14_) | copy-start | bytes 1769476
  52.7 3.6 %collective-permute-start.15 = (f32[3,2,4,24,128]{4,3,2,1,0:T(8,128)}, f32[3,2,4,24,128]{4,3,2,1,0:T(8,128)}, u32[]{:S(2)}, u32[]{:S(2)}) collective-permute-start(f32[3,2,4,24,128]{4,3,2,1,0:T(8,128)} %collective-permute-done.5.refs_11_), channel_id=1, source_target_pairs={{0,1},{1,0},{2,3},{3,2},{4,5},{5,4},{6,7},{7,6},{8,9},{9,8},{10,11... | collective-permute-start | bytes 884744 | tf_op jit(solution)/shard_map/ppermute | solution.py:191
  53.2 1.0 copy-start.7
  54.2 2.1 %collective-permute-start.12 = (f32[3,2,4,24,128]{4,3,2,1,0:T(8,128)}, f32[3,2,4,24,128]{4,3,2,1,0:T(8,128)}, u32[]{:S(2)}, u32[]{:S(2)}) collective-permute-start(f32[3,2,4,24,128]{4,3,2,1,0:T(8,128)} %collective-permute-done.3.refs_8_), channel_id=1, source_target_pairs={{0,1},{1,0},{2,3},{3,2},{4,5},{5,4},{6,7},{7,6},{8,9},{9,8},{10,11... | collective-permute-start | bytes 884744 | tf_op jit(solution)/shard_map/ppermute | solution.py:191
